TPU v7x, 256 devices: a whole 4x4x8 slice. The times are simulated.
256 devices in a mesh: segment: 4 (over x), bins: 64 (over z, y, core).
Axes of the slice: x: 4, y: 4, z: 8, core: 2. Of those that a mesh axis runs over, the one named last changes fastest.
Arguments:
- cube_train: bfloat16 [2, 512, 2048, 256], P(None, None, ('segment', 'bins')), may hold values from -6 to 6
- cube_apply: bfloat16 [2, 512, 2048, 256], P(None, None, ('segment', 'bins')), may hold values from -6 to 6
- hard_bins: int32 [64], replicated, may hold values from 1 to 511, as said below
- easy_bins: int32 [128], replicated, may hold values from 0 to 510, as said below
- stagger: int32 [64, 2], replicated, may hold values from 0 to 127, as said below
- hard_gates: int32 [64, 512], P('bins'), may hold values from 0 to 2047, as said below
- easy_gates: int32 [128, 512], P('bins'), may hold values from 0 to 2047, as said below
Outputs:
- hard_beams: float32 [64, 2, 2048, 128], P('bins', None, 'segment')
- easy_beams: float32 [128, 2, 2048, 128], P('bins', None, 'segment')
Inputs may be any that keep to these rules, and one draw needn't show every extreme that they name: `hard_bins`: 64 distinct bins, none of them among easy_bins. `easy_bins`: 128 distinct bins, none of them among hard_bins. `stagger`: in each row the second offset is larger than the first. `hard_gates`: each row holds 512 distinct range gates. `easy_gates`: each row holds 512 distinct range gates.
All inputs are finite; a program needn't handle non-finite values.
Results may differ from a plain program's by a relative error of at most 0.005.
Values may be sent and summed in bfloat16 or wider, within the bound.
No kernel may reach another device: no remote copies, remote signals or barrier semaphores. Data moves between devices by JAX's collectives and lax.ppermute only.
A program may use at most 64 MiB of HBM per device.

v0:
```python
import functools

import jax
import jax.numpy as jnp
from jax import lax
from jax.experimental import pallas as pl
from jax.experimental.pallas import tpu as pltpu
from jax.sharding import PartitionSpec as P

BEAMS = 128
STEPS = 6
LOADING = 0.5
TWO_PI = 6.283185307179586
MIB = 1024 * 1024


def params(mib):
    return pltpu.CompilerParams(vmem_limit_bytes=mib * MIB)


def vmem():
    return pl.BlockSpec(memory_space=pltpu.VMEM)


def turned(c, s, quarter):
    odd = (quarter & 1) == 1
    a = jnp.where(odd, -s, c)
    b = jnp.where(odd, c, s)
    flip = quarter >= 2
    return jnp.where(flip, -a, a), jnp.where(flip, -b, b)


def doppler_table(hard_bins, easy_bins, stagger, pulses, groups):
    zeros = jnp.zeros((groups,), jnp.int32)
    k = jnp.stack([hard_bins, hard_bins, easy_bins[0::2], easy_bins[1::2]], axis=1)
    d = jnp.stack([stagger[:, 0], stagger[:, 1], zeros, zeros], axis=1)
    k = k.reshape(-1, 1)
    d = d.reshape(-1, 1)
    part = pulses // 4
    lag = jnp.arange(part, dtype=jnp.int32)[None, :] - d
    phase = ((k * lag) & (pulses - 1)).astype(jnp.float32) * (TWO_PI / pulses)
    c0, s0 = jnp.cos(phase), jnp.sin(phase)
    window = lag.astype(jnp.float32) * (TWO_PI / pulses)
    wc, ws = jnp.cos(window), jnp.sin(window)
    window_cos = [wc, -ws, -wc, ws]
    real, imag = [], []
    for a in range(4):
        taper = 0.54 - 0.46 * window_cos[a]
        amplitude = jnp.where(lag + a * part >= 0, taper, 0.0) * 0.0625
        c, s = turned(c0, s0, (k * a) & 3)
        real.append((amplitude * c).astype(jnp.bfloat16))
        imag.append((-amplitude * s).astype(jnp.bfloat16))
    real = jnp.concatenate(real, axis=1)
    imag = jnp.concatenate(imag, axis=1)
    first = jnp.concatenate([real, -imag], axis=1)
    second = jnp.concatenate([imag, real], axis=1)
    return jnp.stack([first, second], axis=1).reshape(-1, 2 * pulses)


def gram_kernel(start_ref, gates_ref, x_ref, hard_ref, easy_ref):
    sources = x_ref.shape[0]
    rows = sources * 16
    row = lax.broadcasted_iota(jnp.int32, (rows, 1), 0)
    gate = (row // 16) * 8 + row % 8 + start_ref[0]
    masks = []
    for which in range(3):
        hit = (gate == gates_ref[which : which + 1, :]).astype(jnp.float32)
        masks.append(jnp.sum(hit, axis=1, keepdims=True))
    plain, masked, turned_ = [], [], []
    for t in range(4):
        x = x_ref[:, t].reshape(rows, -1)
        f = x.astype(jnp.float32)
        f4 = (f * masks[max(t - 1, 0)]).reshape(sources, 2, 8, -1)
        swapped = jnp.concatenate([f4[:, 1:2], -f4[:, 0:1]], axis=1)
        plain.append(x)
        masked.append(f4.reshape(rows, -1).astype(jnp.bfloat16))
        turned_.append(swapped.reshape(rows, -1).astype(jnp.bfloat16))

    def outer(a, b):
        return lax.dot_general(
            a, b, (((0,), (0,)), ((), ())), preferred_element_type=jnp.float32
        )

    def packed(a, m, s):
        order = a.shape[1]
        real, imag = outer(a, m), outer(a, s)
        up = lax.broadcasted_iota(jnp.int32, (order, order), 0) <= lax.broadcasted_iota(
            jnp.int32, (order, order), 1
        )
        return jnp.where(up, real, imag)

    cat = functools.partial(jnp.concatenate, axis=1)
    hard_ref[...] = packed(cat(plain[0:2]), cat(masked[0:2]), cat(turned_[0:2]))
    for e in range(2):
        easy_ref[e] = packed(plain[2 + e], masked[2 + e], turned_[2 + e])


def gram(start, gates, x):
    ch = x.shape[-1]
    return pl.pallas_call(
        gram_kernel,
        out_shape=(
            jax.ShapeDtypeStruct((2 * ch, 2 * ch), jnp.float32),
            jax.ShapeDtypeStruct((2, ch, ch), jnp.float32),
        ),
        in_specs=[pl.BlockSpec(memory_space=pltpu.SMEM), vmem(), vmem()],
        out_specs=(vmem(), vmem()),
        compiler_params=params(40),
        cost_estimate=pl.CostEstimate(
            flops=2 * 10**9, bytes_accessed=4 * MIB, transcendentals=0
        ),
    )(start, gates, x)


def split(x):
    high = x.astype(jnp.bfloat16)
    return high, (x - high.astype(jnp.float32)).astype(jnp.bfloat16)


def solve_one(both, steer, train):
    order = both.shape[0]
    row = lax.broadcasted_iota(jnp.int32, (order, order), 0)
    col = lax.broadcasted_iota(jnp.int32, (order, order), 1)
    both = both * (1.0 / train)
    flipped = both.T
    real = jnp.where(row <= col, both, flipped)
    imag = jnp.where(row > col, both, -flipped)
    imag = jnp.where(row == col, 0.0, imag)
    trace = jnp.sum(jnp.where(row == col, both, 0.0))
    loading = LOADING * trace / order
    highest = loading + trace
    theta = (highest + loading) / 2.0
    delta = (highest - loading) / 2.0
    sigma = theta / delta
    rho = 1.0 / sigma
    real_h, real_l = split(real)
    imag_h, imag_l = split(imag)

    def dot(a, b):
        return jnp.dot(a, b, preferred_element_type=jnp.float32)

    def times(ah, al, bh, bl):
        return dot(ah, bh) + (dot(ah, bl) + dot(al, bh))

    half = steer.shape[1] // 2
    weights = jnp.zeros_like(steer)
    resid = steer
    direction = steer / theta
    for step in range(STEPS):
        weights = weights + direction
        if step + 1 < STEPS:
            dh, dl = split(direction)
            rr = times(real_h, real_l, dh, dl)
            ii = times(imag_h, imag_l, dh, dl)
            product = jnp.concatenate(
                [rr[:, :half] - ii[:, half:], rr[:, half:] + ii[:, :half]], axis=1
            )
            resid = resid - (product + loading * direction)
            rho_next = 1.0 / (2.0 * sigma - rho)
            direction = rho_next * rho * direction + (2.0 * rho_next / delta) * resid
            rho = rho_next
    return weights.astype(jnp.bfloat16)


def solve_kernel(hard_ref, easy_ref, hard_steer_ref, easy_steer_ref, out_ref, *, train):
    ch = easy_ref.shape[1]
    w = solve_one(hard_ref[...], hard_steer_ref[...], train)
    out_ref[0] = w[:ch]
    out_ref[1] = w[ch:]
    for e in range(2):
        out_ref[2 + e] = solve_one(easy_ref[e], easy_steer_ref[...], train)


def solve(hard, easy, hard_steer, easy_steer, train):
    ch = easy.shape[1]
    return pl.pallas_call(
        functools.partial(solve_kernel, train=train),
        out_shape=jax.ShapeDtypeStruct((4, ch, 2 * BEAMS), jnp.bfloat16),
        in_specs=[vmem()] * 4,
        out_specs=vmem(),
        compiler_params=params(40),
        cost_estimate=pl.CostEstimate(
            flops=6 * 10**9, bytes_accessed=3 * MIB, transcendentals=0
        ),
    )(hard, easy, hard_steer, easy_steer)


def steering(bin_value, offsets, channels, pulses):
    channel = jnp.arange(channels, dtype=jnp.int32)
    beam = jnp.arange(BEAMS, dtype=jnp.int32)
    spatial = (channel[:, None] * (beam[None, :] + BEAMS // 2) % BEAMS).astype(
        jnp.float32
    ) * (TWO_PI / BEAMS)
    angles = []
    for offset in offsets:
        temporal = (bin_value * offset % pulses).astype(jnp.float32) * (TWO_PI / pulses)
        angles.append(spatial + temporal)
    angle = jnp.concatenate(angles, axis=0)
    scale = 1.0 / jnp.sqrt(jnp.float32(len(offsets) * channels))
    return jnp.concatenate([jnp.cos(angle), jnp.sin(angle)], axis=1) * scale


def beam_kernel(y_ref, w_ref, hard_ref, easy_ref):
    sources = y_ref.shape[0]
    rows = sources * 16

    def product(t):
        y = y_ref[:, t].reshape(rows, -1)
        return jnp.dot(y, w_ref[t], preferred_element_type=jnp.float32)

    def parts(p):
        p = p.reshape(sources, 2, 8, 2 * BEAMS)
        real = p[:, 0, :, :BEAMS] + p[:, 1, :, BEAMS:]
        imag = p[:, 1, :, :BEAMS] - p[:, 0, :, BEAMS:]
        return real.reshape(sources * 8, BEAMS), imag.reshape(sources * 8, BEAMS)

    hard_ref[0, 0], hard_ref[0, 1] = parts(product(0) + product(1))
    for e in range(2):
        easy_ref[e, 0], easy_ref[e, 1] = parts(product(2 + e))


def beams(y, w, blocks=4):
    sources, _, _, ch = y.shape
    step = sources // blocks
    gates = sources * 8
    return pl.pallas_call(
        beam_kernel,
        grid=(blocks,),
        out_shape=(
            jax.ShapeDtypeStruct((1, 2, gates, BEAMS), jnp.float32),
            jax.ShapeDtypeStruct((2, 2, gates, BEAMS), jnp.float32),
        ),
        in_specs=[
            pl.BlockSpec((step, 4, 16, ch), lambda i: (i, 0, 0, 0)),
            pl.BlockSpec((4, ch, 2 * BEAMS), lambda i: (0, 0, 0)),
        ],
        out_specs=(
            pl.BlockSpec((1, 2, step * 8, BEAMS), lambda i: (0, 0, i, 0)),
            pl.BlockSpec((2, 2, step * 8, BEAMS), lambda i: (0, 0, i, 0)),
        ),
        compiler_params=params(24),
        cost_estimate=pl.CostEstimate(
            flops=5 * 10**8, bytes_accessed=4 * MIB, transcendentals=0
        ),
    )(y, w)


def spectra_of(table, cube, groups):
    pulses, gates, ch = cube.shape[1:]
    flat = cube.reshape(2 * pulses, gates * ch)
    out = jnp.dot(table, flat, preferred_element_type=jnp.float32).astype(jnp.bfloat16)
    return out.reshape(groups, 4, 2 * gates, ch)


def route(spectra):
    return lax.all_to_all(spectra, "bins", split_axis=0, concat_axis=0, tiled=True)


def per_device(cube_train, cube_apply, hard_bins, easy_bins, stagger, hard_gates, easy_gates):
    groups = lax.axis_size("bins")
    section = lax.axis_index("segment")
    group = lax.axis_index("bins")
    pulses = cube_train.shape[1]
    ch = cube_train.shape[3]
    table = doppler_table(hard_bins, easy_bins, stagger, pulses, groups)
    train = route(spectra_of(table, cube_train, groups))
    gates = jnp.concatenate([hard_gates, easy_gates], axis=0)
    start = (section * (groups * 8)).reshape(1).astype(jnp.int32)
    apply_spectra = spectra_of(table, cube_apply, groups)
    train, apply_spectra = lax.optimization_barrier((train, apply_spectra))
    routed = route(apply_spectra)
    hard, easy = gram(start, gates, train)
    both = jnp.concatenate([hard.reshape(-1, ch), easy.reshape(-1, ch)], axis=0)
    both = lax.psum(both, "segment")
    cut = hard.size // ch
    hard = both[:cut].reshape(hard.shape)
    easy = both[cut:].reshape(easy.shape)
    bin_value = hard_bins[group]
    hard_steer = steering(bin_value, [stagger[group, 0], stagger[group, 1]], ch, pulses)
    easy_steer = steering(bin_value, [jnp.zeros((), jnp.int32)], ch, pulses)
    w = solve(hard, easy, hard_steer, easy_steer, hard_gates.shape[1])
    return beams(routed, w)


def solution(mesh):
    in_specs = (
        P(None, None, ("segment", "bins"), None),
        P(None, None, ("segment", "bins"), None),
        P(),
        P(),
        P(),
        P("bins", None),
        P("bins", None),
    )
    out_specs = (P("bins", None, "segment", None), P("bins", None, "segment", None))
    return jax.shard_map(
        per_device, mesh=mesh, in_specs=in_specs, out_specs=out_specs, check_vma=False
    )
```

profile of v0, /device:TPU:6, one launch (start us, length us, event | category | flops | bytes accessed | tf_op | source)
XLA Modules:
  0.0 192.4 jit_solution(6791878486925336013)
XLA Ops:
  7.2 0.8 slice.15
  8.0 0.8 slice.16
  8.8 0.7 pad_add_fusion.1
  9.5 0.1 copy.10
  9.6 0.1 mul.165
  9.7 0.8 copy.12
  10.5 0.1 sub.28
  10.6 1.0 fusion.30
  11.7 1.3 fusion.36
  13.0 1.3 fusion.34
  14.4 1.4 multiply_convert_fusion
  15.8 1.3 fusion.32
  17.2 1.0 fusion.29
  18.1 1.3 fusion.35
  19.5 1.3 fusion.33
  20.8 1.3 fusion.31
  22.2 0.1 pad_maximum_fusion.1
  22.3 1.1 copy.11
  23.4 0.4 reshape.95
  23.9 3.7 %copy.13 = bf16[128,8,8,256]{3,1,2,0:T(8,128)(2,1)S(1)} copy(bf16[128,8,8,256]{3,2,1,0:T(8,128)(2,1)} %bitcast.23) | data formatting | bytes 8388608
  27.6 2.4 %convolution_convert_fusion.1 = bf16[512,2048]{1,0:T(8,128)(2,1)S(1)} fusion(bf16[512,1024]{1,0:T(8,128)(2,1)S(1)} %reshape.95, bf16[1024,2048]{1,0:T(8,128)(2,1)S(1)} %bitcast.26), kind=kOutput, calls=%fused_computation.1 | convolution fusion | flops 2148532224 | bytes 7340032 | tf_op jit(solution)/shard_map/dot_general | solution.py:251
  29.9 2.3 %reshape.97 = bf16[64,4,16,256]{3,2,1,0:T(8,128)(2,1)} reshape(bf16[512,2048]{1,0:T(8,128)(2,1)S(1)} %convolution_convert_fusion.1) | data formatting | bytes 4194304 | tf_op jit(solution)/shard_map/reshape | solution.py:252
  32.3 12.3 %all-to-all-start = ((bf16[64,4,16,256]{3,2,1,0:T(8,128)(2,1)}), bf16[64,4,16,256]{3,2,1,0:T(8,128)(2,1)S(1)}, u32[]{:S(2)}, u32[]{:S(2)}) async-start(bf16[64,4,16,256]{3,2,1,0:T(8,128)(2,1)} %reshape.97), calls=%async_computation | async-start | bytes 4194304 | tf_op jit(solution)/shard_map/all_to_all | solution.py:256
  44.6 3.7 %copy.14 = bf16[128,8,8,256]{3,1,2,0:T(8,128)(2,1)S(1)} copy(bf16[128,8,8,256]{3,2,1,0:T(8,128)(2,1)} %bitcast.24) | data formatting | bytes 8388608
  48.2 3.7 %convolution_convert_fusion = bf16[512,2048]{1,0:T(8,128)(2,1)} fusion(bf16[512,1024]{1,0:T(8,128)(2,1)S(1)} %reshape.95, bf16[1024,2048]{1,0:T(8,128)(2,1)S(1)} %bitcast.25), kind=kOutput, calls=%fused_computation | convolution fusion | flops 2148532224 | bytes 7340032 | tf_op jit(solution)/shard_map/dot_general | solution.py:251
  52.0 4.2 %reshape.99 = bf16[64,4,16,256]{3,2,1,0:T(8,128)(2,1)} reshape(bf16[512,2048]{1,0:T(8,128)(2,1)} %convolution_convert_fusion) | data formatting | bytes 4194304 | tf_op jit(solution)/shard_map/reshape | solution.py:252
  56.2 39.6 %all-to-all-done.x_ref = bf16[64,4,16,256]{3,2,1,0:T(8,128)(2,1)S(1)} async-done(((bf16[64,4,16,256]{3,2,1,0:T(8,128)(2,1)}), bf16[64,4,16,256]{3,2,1,0:T(8,128)(2,1)S(1)}, u32[]{:S(2)}, u32[]{:S(2)}) %all-to-all-start) | async-done | bytes 2097184 | tf_op jit(solution)/shard_map/all_to_all | solution.py:256
  95.7 1.3 copy-done
  97.1 5.3 %all-to-all-start.1 = ((bf16[64,4,16,256]{3,2,1,0:T(8,128)(2,1)}), bf16[64,4,16,256]{3,2,1,0:T(8,128)(2,1)S(1)}, u32[]{:S(2)}, u32[]{:S(2)}) async-start(bf16[64,4,16,256]{3,2,1,0:T(8,128)(2,1)} %reshape.99), calls=%async_computation.1 | async-start | bytes 4194304 | tf_op jit(solution)/shard_map/all_to_all | solution.py:256
  102.5 1.6 copy-done.1
  104.1 2.2 %shard_map.86 = (f32[512,512]{1,0:T(8,128)S(1)}, f32[2,256,256]{2,1,0:T(8,128)S(1)}) custom-call(s32[1]{0:T(128)} %bitcast.5.start_ref, s32[3,512]{1,0:T(4,128)S(1)} %pad_add_fusion.gates_ref, bf16[64,4,16,256]{3,2,1,0:T(8,128)(2,1)S(1)} %copy-done.1), custom_call_target="tpu_custom_call" | custom-call | flops 2000000000 | bytes 4194304 | tf_op jit(solution)/shard_map/pallas_call | solution.py:100
  106.3 0.8 copy-done.5
  107.1 1.1 reshape.101
  108.2 2.7 %pad_maximum_fusion = f32[1536,256]{1,0:T(8,128)} fusion(f32[512,256]{1,0:T(8,128)} %bitcast.22, f32[1024,256]{1,0:T(8,128)} %reshape.101), kind=kLoop, calls=%fused_computation.2 | loop fusion | flops 393216 | bytes 3145728 | tf_op jit(solution)/shard_map/concatenate | solution.py:273
  111.0 0.6 dynamic_slice.9
  111.6 0.6 constant_dynamic-slice_fusion.1
  114.7 0.5 fusion.28
  115.3 0.9 fusion.2
  116.2 0.8 maximum_multiply_fusion.hard_steer_ref
  117.0 49.9 %all-reduce.3.cloned.1.call-done = f32[1536,256]{1,0:T(8,128)} async-done(((f32[1536,256]{1,0:T(8,128)}), f32[1536,256]{1,0:T(8,128)}) %all-reduce.3.cloned.1.call-update) | async-done | bytes 1572880 | tf_op jit(solution)/shard_map/psum | solution.py:274
  166.9 2.3 %slice.19 = f32[1024,256]{1,0:T(8,128)} slice(f32[1536,256]{1,0:T(8,128)} %all-reduce.3.cloned.1.call-done), slice={[0:1024], [0:256]} | slice | bytes 2097152 | tf_op jit(solution)/shard_map/slice | solution.py:276
  169.1 1.5 reshape.103.hard_ref
  170.7 1.1 slice.20
  171.8 1.0 copy-done.4
  172.8 8.5 %shard_map.87.w_ref = bf16[4,256,256]{2,1,0:T(8,128)(2,1)S(1)} custom-call(f32[512,512]{1,0:T(8,128)S(1)} %reshape.103.hard_ref, f32[2,256,256]{2,1,0:T(8,128)S(1)} %bitcast.21, f32[512,256]{1,0:T(8,128)S(1)} %copy-done.4, f32[256,256]{1,0:T(8,128)S(1)} %maximum_multiply_fusion.1.easy_steer_ref), custom_call_target="tpu_custom_call" | custom-call | flops 6000000000 | bytes 3145728 | tf_op jit(solution)/shard_map/pallas_call | solution.py:176
  181.3 0.8 copy-done.2
  182.1 1.0 copy-done.3
  183.2 2.4 %shard_map.88 = (f32[1,2,512,128]{3,2,1,0:T(8,128)}, f32[2,2,512,128]{3,2,1,0:T(8,128)}) custom-call(bf16[64,4,16,256]{3,2,1,0:T(8,128)(2,1)S(1)} %all-to-all-done.1.y_ref, bf16[4,256,256]{2,1,0:T(8,128)(2,1)S(1)} %copy-done.3), custom_call_target="tpu_custom_call" | custom-call | flops 500000000 | bytes 4194304 | tf_op jit(solution)/shard_map/pallas_call | solution.py:226
  (23 shorter events, 0.2 us)
Async XLA Ops:
  32.3 63.5 %all-to-all-start = ((bf16[64,4,16,256]{3,2,1,0:T(8,128)(2,1)}), bf16[64,4,16,256]{3,2,1,0:T(8,128)(2,1)S(1)}, u32[]{:S(2)}, u32[]{:S(2)}) async-start(bf16[64,4,16,256]{3,2,1,0:T(8,128)(2,1)} %reshape.97), calls=%async_computation | async-start | bytes 4194304 | tf_op jit(solution)/shard_map/all_to_all | solution.py:256
  56.2 46.3 %copy-start.6 = (s32[2,512]{1,0:T(2,128)S(1)}, s32[2,512]{1,0:T(2,128)}, u32[]{:S(2)}) copy-start(s32[2,512]{1,0:T(2,128)} %param.13) | copy-start | bytes 12292
  56.2 46.3 %copy-start.8 = (s32[1,512]{1,0:T(1,128)S(1)}, s32[1,512]{1,0:T(1,128)}, u32[]{:S(2)}) copy-start(s32[1,512]{1,0:T(1,128)} %param.12) | copy-start | bytes 6148
  95.7 1.3 copy-start
  97.1 85.1 %all-to-all-start.1 = ((bf16[64,4,16,256]{3,2,1,0:T(8,128)(2,1)}), bf16[64,4,16,256]{3,2,1,0:T(8,128)(2,1)S(1)}, u32[]{:S(2)}, u32[]{:S(2)}) async-start(bf16[64,4,16,256]{3,2,1,0:T(8,128)(2,1)} %reshape.99), calls=%async_computation.1 | async-start | bytes 4194304 | tf_op jit(solution)/shard_map/all_to_all | solution.py:256
  102.4 64.5 %all-reduce.3.cloned.1.call-start = ((), (), s32[]{:S(2)}) async-start(), calls=%async_computation.2 | async-start | bytes 3145728 | tf_op jit(solution)/shard_map/psum | solution.py:274
  102.5 1.6 copy-start.1
  106.3 0.8 copy-start.5
  108.2 2.7 %copy-start.9 = (s32[64]{0:T(128)S(1)}, s32[64]{0:T(128)}, u32[]{:S(2)}) copy-start(s32[64]{0:T(128)} %param.9) | copy-start | bytes 772
  108.2 3.3 %copy-start.7 = (s32[64,2]{0,1:T(2,128)S(1)}, s32[64,2]{0,1:T(2,128)}, u32[]{:S(2)}) copy-start(s32[64,2]{0,1:T(2,128)} %param.11) | copy-start | bytes 1540
  171.8 1.0 copy-start.4
  181.3 0.8 copy-start.2
  182.1 1.0 copy-start.3
Sparse Core Ops, SparseCore 0:
  111.1 55.7 all-reduce.2
where the time goes:
time: 195 us; the launch traced here: 192 us
  waiting for transfers between devices  89.5 us (46%)
  local copies, waits for them, and re-layouts  31.9 us (16%)
  starting transfers between devices  17.7 us (9%)
  other arithmetic  17.4 us (9%)
  between operations  16.8 us (9%)
  Pallas kernels  13.1 us (7%)
  matrix products  6.07 us (3%)
    psum x1, waiting for transfers between devices, per_device(): both = lax.psum(both, 'segment')  49.9 us
    all_to_all x2, waiting for transfers between devices, route(): lax.all_to_all(spectra, 'bins', split_axis=0, concat_axis=0, tiled=True)  39.6 us
    all_to_all x2, starting transfers between devices, route(): lax.all_to_all(spectra, 'bins', split_axis=0, concat_axis=0, tiled=True)  17.6 us
    unnamed x23, local copies, waits for them, and re-layouts  14.7 us
    unnamed x7, other arithmetic  8.72 us
    pallas_call x1, Pallas kernels, solve(): pl.pallas_call(functools.partial(solve_kernel, train=train), out_shape=ja...  8.5 us
    reshape x2, local copies, waits for them, and re-layouts, spectra_of(): return out.reshape(groups, 4, 2 * gates, ch)  6.56 us
    dot_general x2, matrix products, spectra_of(): jnp.dot(table, flat, preferred_element_type=jnp.float32)  6.07 us
  transfers between devices with their start and end apart: 3, of which 2 were waited for; matrix products, arithmetic and copies ran while one was open for 12% of the time, Pallas kernels for 6%

commit v1 on v0

--- a/solution.py
+++ b/solution.py
@@ -30,38 +30,72 @@
     return jnp.where(flip, -a, a), jnp.where(flip, -b, b)
 
 
-def doppler_table(hard_bins, easy_bins, stagger, pulses, groups):
-    zeros = jnp.zeros((groups,), jnp.int32)
-    k = jnp.stack([hard_bins, hard_bins, easy_bins[0::2], easy_bins[1::2]], axis=1)
-    d = jnp.stack([stagger[:, 0], stagger[:, 1], zeros, zeros], axis=1)
-    k = k.reshape(-1, 1)
-    d = d.reshape(-1, 1)
+def iota(shape, dim):
+    return lax.broadcasted_iota(jnp.int32, shape, dim)
+
+
+def table_kernel(hard_ref, easy_ref, stagger_ref, out_ref):
+    pulses = out_ref.shape[3] // 2
+    groups = hard_ref.shape[1]
+    rows = 4 * groups
     part = pulses // 4
-    lag = jnp.arange(part, dtype=jnp.int32)[None, :] - d
+    group = iota((rows, 1), 0) // 4
+    t = iota((rows, 1), 0) % 4
+
+    def picked(ref, index):
+        at = iota((rows, ref.shape[1]), 1) == index
+        return jnp.sum(jnp.where(at, ref[...], 0), axis=1, keepdims=True)
+
+    k = jnp.where(t < 2, picked(hard_ref, group), picked(easy_ref, 2 * group + t - 2))
+    spread = (iota((rows, groups), 1) == iota((rows, groups), 0) // 4).astype(jnp.float32)
+    both = jnp.dot(
+        spread.astype(jnp.bfloat16),
+        stagger_ref[...].astype(jnp.float32).astype(jnp.bfloat16),
+        preferred_element_type=jnp.float32,
+    ).astype(jnp.int32)
+    d = jnp.where(t == 0, both[:, 0:1], jnp.where(t == 1, both[:, 1:2], 0))
+    lag = iota((rows, part), 1) - d
     phase = ((k * lag) & (pulses - 1)).astype(jnp.float32) * (TWO_PI / pulses)
     c0, s0 = jnp.cos(phase), jnp.sin(phase)
     window = lag.astype(jnp.float32) * (TWO_PI / pulses)
     wc, ws = jnp.cos(window), jnp.sin(window)
-    window_cos = [wc, -ws, -wc, ws]
-    real, imag = [], []
-    for a in range(4):
-        taper = 0.54 - 0.46 * window_cos[a]
+    for a, window_cos in enumerate([wc, -ws, -wc, ws]):
+        taper = 0.54 - 0.46 * window_cos
         amplitude = jnp.where(lag + a * part >= 0, taper, 0.0) * 0.0625
         c, s = turned(c0, s0, (k * a) & 3)
-        real.append((amplitude * c).astype(jnp.bfloat16))
-        imag.append((-amplitude * s).astype(jnp.bfloat16))
-    real = jnp.concatenate(real, axis=1)
-    imag = jnp.concatenate(imag, axis=1)
-    first = jnp.concatenate([real, -imag], axis=1)
-    second = jnp.concatenate([imag, real], axis=1)
-    return jnp.stack([first, second], axis=1).reshape(-1, 2 * pulses)
-
-
-def gram_kernel(start_ref, gates_ref, x_ref, hard_ref, easy_ref):
+        shape = (groups // 8, 32, part)
+        real = (amplitude * c).reshape(shape)
+        imag = (amplitude * s).reshape(shape)
+        low = slice(a * part, (a + 1) * part)
+        high = slice(pulses + a * part, pulses + (a + 1) * part)
+        out_ref[:, 0, :, low] = real.astype(jnp.bfloat16)
+        out_ref[:, 0, :, high] = imag.astype(jnp.bfloat16)
+        out_ref[:, 1, :, low] = (-imag).astype(jnp.bfloat16)
+        out_ref[:, 1, :, high] = real.astype(jnp.bfloat16)
+
+
+def doppler_table(hard_bins, easy_bins, stagger, pulses, groups):
+    out = pl.pallas_call(
+        table_kernel,
+        out_shape=jax.ShapeDtypeStruct((groups // 8, 2, 32, 2 * pulses), jnp.bfloat16),
+        in_specs=[vmem()] * 3,
+        out_specs=vmem(),
+        compiler_params=params(24),
+        cost_estimate=pl.CostEstimate(
+            flops=10**7, bytes_accessed=MIB, transcendentals=200000
+        ),
+    )(hard_bins.reshape(1, -1), easy_bins.reshape(1, -1), stagger)
+    return out.reshape(-1, 2 * pulses)
+
+
+def gram_kernel(section_ref, gates_ref, x_ref, *refs, train):
+    outs, scratch = refs[:-1], refs[-1]
+    section = section_ref[0]
+    start = section * (x_ref.shape[0] * 8)
     sources = x_ref.shape[0]
     rows = sources * 16
     row = lax.broadcasted_iota(jnp.int32, (rows, 1), 0)
-    gate = (row // 16) * 8 + row % 8 + start_ref[0]
+    gate = (row // 16) * 8 + row % 8 + start
     masks = []
     for which in range(3):
         hit = (gate == gates_ref[which : which + 1, :]).astype(jnp.float32)
@@ -87,29 +121,36 @@
         up = lax.broadcasted_iota(jnp.int32, (order, order), 0) <= lax.broadcasted_iota(
             jnp.int32, (order, order), 1
         )
-        return jnp.where(up, real, imag)
+        return (jnp.where(up, real, imag) * (1.0 / train)).astype(jnp.bfloat16)
 
     cat = functools.partial(jnp.concatenate, axis=1)
-    hard_ref[...] = packed(cat(plain[0:2]), cat(masked[0:2]), cat(turned_[0:2]))
-    for e in range(2):
-        easy_ref[e] = packed(plain[2 + e], masked[2 + e], turned_[2 + e])
-
-
-def gram(start, gates, x):
+    ch = x_ref.shape[-1]
+    hard = packed(cat(plain[0:2]), cat(masked[0:2]), cat(turned_[0:2]))
+    full = jnp.concatenate(
+        [hard[:, :ch], hard[:, ch:]]
+        + [packed(plain[2 + e], masked[2 + e], turned_[2 + e]) for e in range(2)],
+        axis=0,
+    )
+    scratch[...] = full.reshape(scratch.shape)
+    sections = len(outs)
+    for shift, out in enumerate(outs):
+        out[...] = scratch[(section + shift) % sections]
+
+
+def gram(section, gates, x, sections):
     ch = x.shape[-1]
+    block = (6 * ch // sections, ch)
     return pl.pallas_call(
-        gram_kernel,
-        out_shape=(
-            jax.ShapeDtypeStruct((2 * ch, 2 * ch), jnp.float32),
-            jax.ShapeDtypeStruct((2, ch, ch), jnp.float32),
-        ),
+        functools.partial(gram_kernel, train=gates.shape[1]),
+        out_shape=[jax.ShapeDtypeStruct(block, jnp.bfloat16)] * sections,
         in_specs=[pl.BlockSpec(memory_space=pltpu.SMEM), vmem(), vmem()],
-        out_specs=(vmem(), vmem()),
+        out_specs=[vmem()] * sections,
+        scratch_shapes=[pltpu.VMEM((sections, *block), jnp.bfloat16)],
         compiler_params=params(40),
         cost_estimate=pl.CostEstimate(
             flops=2 * 10**9, bytes_accessed=4 * MIB, transcendentals=0
         ),
-    )(start, gates, x)
+    )(section, gates, x)
 
 
 def split(x):
@@ -117,11 +158,10 @@
     return high, (x - high.astype(jnp.float32)).astype(jnp.bfloat16)
 
 
-def solve_one(both, steer, train):
+def solve_one(both, steer):
     order = both.shape[0]
     row = lax.broadcasted_iota(jnp.int32, (order, order), 0)
     col = lax.broadcasted_iota(jnp.int32, (order, order), 1)
-    both = both * (1.0 / train)
     flipped = both.T
     real = jnp.where(row <= col, both, flipped)
     imag = jnp.where(row > col, both, -flipped)
@@ -133,14 +173,11 @@
     delta = (highest - loading) / 2.0
     sigma = theta / delta
     rho = 1.0 / sigma
-    real_h, real_l = split(real)
-    imag_h, imag_l = split(imag)
+    real = real.astype(jnp.bfloat16)
+    imag = imag.astype(jnp.bfloat16)
 
     def dot(a, b):
         return jnp.dot(a, b, preferred_element_type=jnp.float32)
-
-    def times(ah, al, bh, bl):
-        return dot(ah, bh) + (dot(ah, bl) + dot(al, bh))
 
     half = steer.shape[1] // 2
     weights = jnp.zeros_like(steer)
@@ -150,8 +187,8 @@
         weights = weights + direction
         if step + 1 < STEPS:
             dh, dl = split(direction)
-            rr = times(real_h, real_l, dh, dl)
-            ii = times(imag_h, imag_l, dh, dl)
+            rr = dot(real, dh) + dot(real, dl)
+            ii = dot(imag, dh) + dot(imag, dl)
             product = jnp.concatenate(
                 [rr[:, :half] - ii[:, half:], rr[:, half:] + ii[:, :half]], axis=1
             )
@@ -162,27 +199,35 @@
     return weights.astype(jnp.bfloat16)
 
 
-def solve_kernel(hard_ref, easy_ref, hard_steer_ref, easy_steer_ref, out_ref, *, train):
-    ch = easy_ref.shape[1]
-    w = solve_one(hard_ref[...], hard_steer_ref[...], train)
+def solve_kernel(section_ref, *refs):
+    parts, (hard_steer_ref, easy_steer_ref, out_ref, scratch) = refs[:-4], refs[-4:]
+    sections = len(parts)
+    for shift, part in enumerate(parts):
+        scratch[(section_ref[0] + sections - shift) % sections] = part[...]
+    ch = out_ref.shape[1]
+    full = scratch[...].reshape(6 * ch, ch).astype(jnp.float32)
+    hard = jnp.concatenate([full[: 2 * ch], full[2 * ch : 4 * ch]], axis=1)
+    w = solve_one(hard, hard_steer_ref[...])
     out_ref[0] = w[:ch]
     out_ref[1] = w[ch:]
     for e in range(2):
-        out_ref[2 + e] = solve_one(easy_ref[e], easy_steer_ref[...], train)
-
-
-def solve(hard, easy, hard_steer, easy_steer, train):
-    ch = easy.shape[1]
+        easy = full[(4 + e) * ch : (5 + e) * ch]
+        out_ref[2 + e] = solve_one(easy, easy_steer_ref[...])
+
+
+def solve(section, parts, hard_steer, easy_steer):
+    ch = parts[0].shape[1]
     return pl.pallas_call(
-        functools.partial(solve_kernel, train=train),
+        solve_kernel,
         out_shape=jax.ShapeDtypeStruct((4, ch, 2 * BEAMS), jnp.bfloat16),
-        in_specs=[vmem()] * 4,
+        in_specs=[pl.BlockSpec(memory_space=pltpu.SMEM)] + [vmem()] * (len(parts) + 2),
         out_specs=vmem(),
+        scratch_shapes=[pltpu.VMEM((len(parts), *parts[0].shape), jnp.bfloat16)],
         compiler_params=params(40),
         cost_estimate=pl.CostEstimate(
             flops=6 * 10**9, bytes_accessed=3 * MIB, transcendentals=0
         ),
-    )(hard, easy, hard_steer, easy_steer)
+    )(section, *parts, hard_steer, easy_steer)
 
 
 def steering(bin_value, offsets, channels, pulses):
@@ -249,11 +294,17 @@
     pulses, gates, ch = cube.shape[1:]
     flat = cube.reshape(2 * pulses, gates * ch)
     out = jnp.dot(table, flat, preferred_element_type=jnp.float32).astype(jnp.bfloat16)
-    return out.reshape(groups, 4, 2 * gates, ch)
+    out = out.reshape(groups // 8, 2, 8, 4, gates, ch)
+    return jnp.transpose(out, (0, 2, 3, 1, 4, 5)).reshape(groups, 4, 2 * gates, ch)
 
 
 def route(spectra):
     return lax.all_to_all(spectra, "bins", split_axis=0, concat_axis=0, tiled=True)
+
+
+def shifted(x, by):
+    size = lax.axis_size("segment")
+    return lax.ppermute(x, "segment", [(i, (i + by) % size) for i in range(size)])
 
 
 def per_device(cube_train, cube_apply, hard_bins, easy_bins, stagger, hard_gates, easy_gates):
@@ -265,20 +316,19 @@
     table = doppler_table(hard_bins, easy_bins, stagger, pulses, groups)
     train = route(spectra_of(table, cube_train, groups))
     gates = jnp.concatenate([hard_gates, easy_gates], axis=0)
-    start = (section * (groups * 8)).reshape(1).astype(jnp.int32)
     apply_spectra = spectra_of(table, cube_apply, groups)
     train, apply_spectra = lax.optimization_barrier((train, apply_spectra))
     routed = route(apply_spectra)
-    hard, easy = gram(start, gates, train)
-    both = jnp.concatenate([hard.reshape(-1, ch), easy.reshape(-1, ch)], axis=0)
-    both = lax.psum(both, "segment")
-    cut = hard.size // ch
-    hard = both[:cut].reshape(hard.shape)
-    easy = both[cut:].reshape(easy.shape)
+    sections = lax.axis_size("segment")
+    where = section.reshape(1).astype(jnp.int32)
+    parts = gram(where, gates, train, sections)
+    arrived = [parts[0]] + [shifted(parts[d], d) for d in range(1, sections)]
+    own = sum(p.astype(jnp.float32) for p in arrived).astype(jnp.bfloat16)
+    parts = [own] + [shifted(own, d) for d in range(1, sections)]
     bin_value = hard_bins[group]
     hard_steer = steering(bin_value, [stagger[group, 0], stagger[group, 1]], ch, pulses)
     easy_steer = steering(bin_value, [jnp.zeros((), jnp.int32)], ch, pulses)
-    w = solve(hard, easy, hard_steer, easy_steer, hard_gates.shape[1])
+    w = solve(where, parts, hard_steer, easy_steer)
     return beams(routed, w)
 
 

time: 195 us -> 136 us (0.70)
  waiting for transfers between devices: 89.5 us -> 70.6 us
  other arithmetic: 17.4 us -> 1.64 us
  local copies, waits for them, and re-layouts: 31.9 us -> 16.7 us
  between operations: 16.8 us -> 3.44 us
  starting transfers between devices: 17.7 us -> 25.2 us
    psum x1 -> x0, waiting for transfers between devices: 49.9 us -> none  [per_device(): both = lax.psum(both, 'segment')]
    ppermute x0 -> x6, waiting for transfers between devices: none -> 18.3 us  [shifted(): lax.ppermute(x, 'segment', [(i, (i + by) % size) for i in range(size)])]
    all_to_all x2, waiting for transfers between devices: 39.6 us -> 52.2 us  [route(): lax.all_to_all(spectra, 'bins', split_axis=0, concat_axis=0, tiled=True)]
    unnamed x7 -> x0, other arithmetic: 8.72 us -> none
    ppermute x0 -> x6, starting transfers between devices: none -> 7.79 us  [shifted(): lax.ppermute(x, 'segment', [(i, (i + by) % size) for i in range(size)])]
    reshape x5 -> x2, local copies, waits for them, and re-layouts: 9.66 us -> 3.01 us  [spectra_of(): out = out.reshape(groups // 8, 2, 8, 4, gates, ch)]
    slice x4 -> x0, local copies, waits for them, and re-layouts: 4.95 us -> none  [the longest x1 2.26 us: per_device(): hard = both[:cut].reshape(hard.shape)]
    concatenate x3 -> x0, other arithmetic: 4.08 us -> none  [the longest x1 2.69 us: per_device(): both = jnp.concatenate([hard.reshape(-1, ch), easy.reshape(-1, ch)], axis=0)]
  transfers between devices with their start and end apart: 3 -> 8, of which waited for: 2 -> 7; matrix products, arithmetic and copies ran while one was open for 12% -> 8% of each run, Pallas kernels for 6% -> 7%
where the time goes in v1:
time: 136 us; the launch traced here: 135 us
  waiting for transfers between devices  70.6 us (52%)
  starting transfers between devices  25.2 us (19%)
  local copies, waits for them, and re-layouts  16.7 us (12%)
  Pallas kernels  13 us (10%)
  matrix products  4.74 us (3%)
  between operations  3.44 us (3%)
  other arithmetic  1.64 us (1%)
    all_to_all x2, waiting for transfers between devices, route(): lax.all_to_all(spectra, 'bins', split_axis=0, concat_axis=0, tiled=True)  52.2 us
    ppermute x6, waiting for transfers between devices, shifted(): lax.ppermute(x, 'segment', [(i, (i + by) % size) for i in range(size)])  18.3 us
    all_to_all x2, starting transfers between devices, route(): lax.all_to_all(spectra, 'bins', split_axis=0, concat_axis=0, tiled=True)  17.4 us
    unnamed x19, local copies, waits for them, and re-layouts  12.4 us
    ppermute x6, starting transfers between devices, shifted(): lax.ppermute(x, 'segment', [(i, (i + by) % size) for i in range(size)])  7.79 us
    pallas_call x1, Pallas kernels, solve(): pl.pallas_call(solve_kernel, out_shape=jax.ShapeDtypeStruct((4, ch, 2 * B...  6.56 us
    dot_general x2, matrix products, spectra_of(): jnp.dot(table, flat, preferred_element_type=jnp.float32)  4.74 us
    reshape x2, local copies, waits for them, and re-layouts, spectra_of(): out = out.reshape(groups // 8, 2, 8, 4, gates, ch)  3.01 us
  transfers between devices with their start and end apart: 8, of which 7 were waited for; matrix products, arithmetic and copies ran while one was open for 8% of the time, Pallas kernels for 7%

profile of v1, /device:TPU:6, one launch (start us, length us, event | category | flops | bytes accessed | tf_op | source)
XLA Modules:
  0.0 135.2 jit_solution(4980893351212910617)
XLA Ops:
  0.6 0.8 copy.9.stagger_ref
  1.4 0.0 copy-start.2
  1.4 0.0 copy-start.3
  1.4 3.7 %copy.12 = bf16[128,8,8,256]{3,1,2,0:T(8,128)(2,1)S(1)} copy(bf16[128,8,8,256]{3,2,1,0:T(8,128)(2,1)} %bitcast.37) | data formatting | bytes 8388608
  5.1 0.0 copy-done.2
  5.1 0.0 copy-done.3
  5.1 1.6 %shard_map.86 = bf16[8,2,32,1024]{3,2,1,0:T(8,128)(2,1)S(1)} custom-call(s32[1,64]{1,0:T(1,128)S(1)} %bitcast.32, s32[1,128]{1,0:T(1,128)S(1)} %bitcast.31, s32[64,2]{1,0:T(8,128)S(1)} %copy.9.stagger_ref), custom_call_target="tpu_custom_call" | custom-call | flops 10000000 | bytes 1048576 | tf_op jit(solution)/shard_map/pallas_call | solution.py:78
  6.7 2.4 %convolution_convert_fusion.1 = bf16[512,2048]{1,0:T(8,128)(2,1)S(1)} fusion(bf16[512,1024]{1,0:T(8,128)(2,1)S(1)} %bitcast.29, bf16[1024,2048]{1,0:T(8,128)(2,1)S(1)} %bitcast.39), kind=kOutput, calls=%fused_computation.1 | convolution fusion | flops 2148532224 | bytes 7340032 | tf_op jit(solution)/shard_map/dot_general | solution.py:296
  9.1 0.7 copy.13
  9.8 1.5 %copy.10 = bf16[8,2,8,4,8,256]{5,4,1,3,2,0:T(8,128)(2,1)} copy(bf16[8,2,8,4,8,256]{5,4,3,2,1,0:T(8,128)(2,1)S(1)} %bitcast.35) | data formatting | bytes 4194304 | tf_op jit(solution)/shard_map/reshape | solution.py:297
  11.3 12.1 %all-to-all-start = ((bf16[64,4,16,256]{3,2,1,0:T(8,128)(2,1)}), bf16[64,4,16,256]{3,2,1,0:T(8,128)(2,1)S(1)}, u32[]{:S(2)}, u32[]{:S(2)}) async-start(bf16[64,4,16,256]{3,2,1,0:T(8,128)(2,1)} %bitcast.34), calls=%async_computation | async-start | bytes 4194304 | tf_op jit(solution)/shard_map/all_to_all | solution.py:302
  23.4 3.7 %copy.14 = bf16[128,8,8,256]{3,1,2,0:T(8,128)(2,1)S(1)} copy(bf16[128,8,8,256]{3,2,1,0:T(8,128)(2,1)} %bitcast.38) | data formatting | bytes 8388608
  27.1 2.4 %convolution_convert_fusion = bf16[512,2048]{1,0:T(8,128)(2,1)S(1)} fusion(bf16[512,1024]{1,0:T(8,128)(2,1)S(1)} %bitcast.30, bf16[1024,2048]{1,0:T(8,128)(2,1)S(1)} %bitcast.40), kind=kOutput, calls=%fused_computation | convolution fusion | flops 2148532224 | bytes 7340032 | tf_op jit(solution)/shard_map/dot_general | solution.py:296
  29.5 0.7 copy.15
  30.2 0.0 copy-start.5
  30.2 0.0 copy-start.4
  30.2 0.0 copy-start.6
  30.2 1.5 %copy.11 = bf16[8,2,8,4,8,256]{5,4,1,3,2,0:T(8,128)(2,1)} copy(bf16[8,2,8,4,8,256]{5,4,3,2,1,0:T(8,128)(2,1)S(1)} %bitcast.36) | data formatting | bytes 4194304 | tf_op jit(solution)/shard_map/reshape | solution.py:297
  31.7 43.1 %all-to-all-done.x_ref = bf16[64,4,16,256]{3,2,1,0:T(8,128)(2,1)S(1)} async-done(((bf16[64,4,16,256]{3,2,1,0:T(8,128)(2,1)}), bf16[64,4,16,256]{3,2,1,0:T(8,128)(2,1)S(1)}, u32[]{:S(2)}, u32[]{:S(2)}) %all-to-all-start) | async-done | bytes 2097184 | tf_op jit(solution)/shard_map/all_to_all | solution.py:302
  74.8 1.3 copy-done
  76.1 5.3 %all-to-all-start.1 = ((bf16[64,4,16,256]{3,2,1,0:T(8,128)(2,1)}), bf16[64,4,16,256]{3,2,1,0:T(8,128)(2,1)S(1)}, u32[]{:S(2)}, u32[]{:S(2)}) async-start(bf16[64,4,16,256]{3,2,1,0:T(8,128)(2,1)} %bitcast.33), calls=%async_computation.1 | async-start | bytes 4194304 | tf_op jit(solution)/shard_map/all_to_all | solution.py:302
  81.4 0.6 dynamic_slice.9
  82.0 0.0 copy-done.5
  82.0 0.7 constant_dynamic-slice_fusion.1
  85.3 0.0 copy-done.4
  85.3 0.0 copy-done.6
  85.3 0.0 copy-start.1
  85.3 1.6 %copy-done.1 = bf16[64,4,16,256]{3,2,1,0:T(8,128)(2,1)S(1)} copy-done((bf16[64,4,16,256]{3,2,1,0:T(8,128)(2,1)S(1)}, bf16[64,4,16,256]{3,2,1,0:T(8,128)(2,1)}, u32[]{:S(2)}) %copy-start.1) | copy-done | bytes 2097176
  86.9 2.4 %shard_map.87 = (bf16[384,256]{1,0:T(8,128)(2,1)S(1)}, bf16[384,256]{1,0:T(8,128)(2,1)S(1)}, bf16[384,256]{1,0:T(8,128)(2,1)S(1)}, bf16[384,256]{1,0:T(8,128)(2,1)S(1)}) custom-call(s32[1]{0:T(128)} %bitcast.7.section_ref, s32[3,512]{1,0:T(4,128)S(1)} %pad_add_fusion.gates_ref, bf16[64,4,16,256]{3,2,1,0:T(8,128)(2,1)S(1)} %copy-done.1), custom_call_target="tpu_custom_call" | custom-call | flops 2000000000 | bytes 4194304 | tf_op jit(solution)/shard_map/pallas_call | solution.py:143
  89.3 0.9 collective-permute-start.2
  90.2 1.1 collective-permute-start.1
  91.3 2.1 %collective-permute-start = (bf16[384,256]{1,0:T(8,128)(2,1)S(1)}, bf16[384,256]{1,0:T(8,128)(2,1)S(1)}, u32[]{:S(2)}, u32[]{:S(2)}) collective-permute-start(bf16[384,256]{1,0:T(8,128)(2,1)S(1)} %get-tuple-element.11), channel_id=1, source_target_pairs={{0,64},{64,128},{128,192},{192,0},{1,65},{65,129},{129,193},{193,1... | collective-permute-start | bytes 589832 | tf_op jit(solution)/shard_map/ppermute | solution.py:307
  93.4 0.5 fusion.9
  94.0 0.9 fusion.1
  94.9 6.8 %collective-permute-done.2 = bf16[384,256]{1,0:T(8,128)(2,1)S(1)} collective-permute-done((bf16[384,256]{1,0:T(8,128)(2,1)S(1)}, bf16[384,256]{1,0:T(8,128)(2,1)S(1)}, u32[]{:S(2)}, u32[]{:S(2)}) %collective-permute-start.2) | collective-permute-done | bytes 196640 | tf_op jit(solution)/shard_map/ppermute | solution.py:307
  101.7 0.0 collective-permute-done.1
  101.7 0.6 collective-permute-done
  102.3 0.1 add_convert_fusion.refs_0_
  102.4 2.7 %collective-permute-start.3 = (bf16[384,256]{1,0:T(8,128)(2,1)S(1)}, bf16[384,256]{1,0:T(8,128)(2,1)S(1)}, u32[]{:S(2)}, u32[]{:S(2)}) collective-permute-start(bf16[384,256]{1,0:T(8,128)(2,1)S(1)} %add_convert_fusion.refs_0_), channel_id=1, source_target_pairs={{0,64},{64,128},{128,192},{192,0},{1,65},{65,129},{129,193},{193,1... | collective-permute-start | bytes 589832 | tf_op jit(solution)/shard_map/ppermute | solution.py:307
  105.1 0.2 collective-permute-start.4
  105.3 0.8 collective-permute-start.5
  106.1 0.1 maximum_multiply_fusion.refs_4_
  106.1 7.5 %collective-permute-done.3.refs_1_ = bf16[384,256]{1,0:T(8,128)(2,1)S(1)} collective-permute-done((bf16[384,256]{1,0:T(8,128)(2,1)S(1)}, bf16[384,256]{1,0:T(8,128)(2,1)S(1)}, u32[]{:S(2)}, u32[]{:S(2)}) %collective-permute-start.3) | collective-permute-done | bytes 196640 | tf_op jit(solution)/shard_map/ppermute | solution.py:307
  113.7 0.8 collective-permute-done.4.refs_2_
  114.4 2.7 %collective-permute-done.5.refs_3_ = bf16[384,256]{1,0:T(8,128)(2,1)S(1)} collective-permute-done((bf16[384,256]{1,0:T(8,128)(2,1)S(1)}, bf16[384,256]{1,0:T(8,128)(2,1)S(1)}, u32[]{:S(2)}, u32[]{:S(2)}) %collective-permute-start.5) | collective-permute-done | bytes 196640 | tf_op jit(solution)/shard_map/ppermute | solution.py:307
  117.1 6.6 %shard_map.88.w_ref = bf16[4,256,256]{2,1,0:T(8,128)(2,1)S(1)} custom-call(s32[1]{0:T(128)} %bitcast.7.section_ref, bf16[384,256]{1,0:T(8,128)(2,1)S(1)} %add_convert_fusion.refs_0_, bf16[384,256]{1,0:T(8,128)(2,1)S(1)} %collective-permute-done.3.refs_1_, bf16[384,256]{1,0:T(8,128)(2,1)S(1)} %collective-permute-done.4.refs_2_, ...), custom_call_target="tpu_custom_call" | custom-call | flops 6000000000 | bytes 3145728 | tf_op jit(solution)/shard_map/pallas_call | solution.py:220
  123.6 9.1 %all-to-all-done.1.y_ref = bf16[64,4,16,256]{3,2,1,0:T(8,128)(2,1)S(1)} async-done(((bf16[64,4,16,256]{3,2,1,0:T(8,128)(2,1)}), bf16[64,4,16,256]{3,2,1,0:T(8,128)(2,1)S(1)}, u32[]{:S(2)}, u32[]{:S(2)}) %all-to-all-start.1) | async-done | bytes 2097184 | tf_op jit(solution)/shard_map/all_to_all | solution.py:302
  132.8 2.4 %shard_map.89 = (f32[1,2,512,128]{3,2,1,0:T(8,128)}, f32[2,2,512,128]{3,2,1,0:T(8,128)}) custom-call(bf16[64,4,16,256]{3,2,1,0:T(8,128)(2,1)S(1)} %all-to-all-done.1.y_ref, bf16[4,256,256]{2,1,0:T(8,128)(2,1)S(1)} %shard_map.88.w_ref), custom_call_target="tpu_custom_call" | custom-call | flops 500000000 | bytes 4194304 | tf_op jit(solution)/shard_map/pallas_call | solution.py:271
  (4 shorter events, 0.0 us)
Async XLA Ops:
  1.4 3.7 %copy-start.2 = (s32[128]{0:T(128)S(1)}, s32[128]{0:T(128)}, u32[]{:S(2)}) copy-start(s32[128]{0:T(128)} %param.10) | copy-start | bytes 1540
  1.4 3.7 %copy-start.3 = (s32[64]{0:T(128)S(1)}, s32[64]{0:T(128)}, u32[]{:S(2)}) copy-start(s32[64]{0:T(128)} %param.9) | copy-start | bytes 772
  11.3 63.5 %all-to-all-start = ((bf16[64,4,16,256]{3,2,1,0:T(8,128)(2,1)}), bf16[64,4,16,256]{3,2,1,0:T(8,128)(2,1)S(1)}, u32[]{:S(2)}, u32[]{:S(2)}) async-start(bf16[64,4,16,256]{3,2,1,0:T(8,128)(2,1)} %bitcast.34), calls=%async_computation | async-start | bytes 4194304 | tf_op jit(solution)/shard_map/all_to_all | solution.py:302
  30.2 51.9 %copy-start.5 = (s32[64,2]{0,1:T(2,128)S(1)}, s32[64,2]{0,1:T(2,128)}, u32[]{:S(2)}) copy-start(s32[64,2]{0,1:T(2,128)} %param.11) | copy-start | bytes 1540
  30.2 55.1 %copy-start.4 = (s32[2,512]{1,0:T(2,128)S(1)}, s32[2,512]{1,0:T(2,128)}, u32[]{:S(2)}) copy-start(s32[2,512]{1,0:T(2,128)} %param.13) | copy-start | bytes 12292
  30.2 55.1 %copy-start.6 = (s32[1,512]{1,0:T(1,128)S(1)}, s32[1,512]{1,0:T(1,128)}, u32[]{:S(2)}) copy-start(s32[1,512]{1,0:T(1,128)} %param.12) | copy-start | bytes 6148
  74.8 1.3 copy-start
  76.1 56.7 %all-to-all-start.1 = ((bf16[64,4,16,256]{3,2,1,0:T(8,128)(2,1)}), bf16[64,4,16,256]{3,2,1,0:T(8,128)(2,1)S(1)}, u32[]{:S(2)}, u32[]{:S(2)}) async-start(bf16[64,4,16,256]{3,2,1,0:T(8,128)(2,1)} %bitcast.33), calls=%async_computation.1 | async-start | bytes 4194304 | tf_op jit(solution)/shard_map/all_to_all | solution.py:302
  85.3 1.6 %copy-start.1 = (bf16[64,4,16,256]{3,2,1,0:T(8,128)(2,1)S(1)}, bf16[64,4,16,256]{3,2,1,0:T(8,128)(2,1)}, u32[]{:S(2)}) copy-start(bf16[64,4,16,256]{3,2,1,0:T(8,128)(2,1)} %copy-done) | copy-start | bytes 6291460
  89.3 12.4 %collective-permute-start.2 = (bf16[384,256]{1,0:T(8,128)(2,1)S(1)}, bf16[384,256]{1,0:T(8,128)(2,1)S(1)}, u32[]{:S(2)}, u32[]{:S(2)}) collective-permute-start(bf16[384,256]{1,0:T(8,128)(2,1)S(1)} %get-tuple-element.13), channel_id=1, source_target_pairs={{0,192},{64,0},{128,64},{192,128},{1,193},{65,1},{129,65},{193,129... | collective-permute-start | bytes 589832 | tf_op jit(solution)/shard_map/ppermute | solution.py:307
  90.2 11.5 %collective-permute-start.1 = (bf16[384,256]{1,0:T(8,128)(2,1)S(1)}, bf16[384,256]{1,0:T(8,128)(2,1)S(1)}, u32[]{:S(2)}, u32[]{:S(2)}) collective-permute-start(bf16[384,256]{1,0:T(8,128)(2,1)S(1)} %get-tuple-element.12), channel_id=1, source_target_pairs={{0,128},{64,192},{128,0},{192,64},{1,129},{65,193},{129,1},{193,65... | collective-permute-start | bytes 589832 | tf_op jit(solution)/shard_map/ppermute | solution.py:307
  91.3 11.0 %collective-permute-start = (bf16[384,256]{1,0:T(8,128)(2,1)S(1)}, bf16[384,256]{1,0:T(8,128)(2,1)S(1)}, u32[]{:S(2)}, u32[]{:S(2)}) collective-permute-start(bf16[384,256]{1,0:T(8,128)(2,1)S(1)} %get-tuple-element.11), channel_id=1, source_target_pairs={{0,64},{64,128},{128,192},{192,0},{1,65},{65,129},{129,193},{193,1... | collective-permute-start | bytes 589832 | tf_op jit(solution)/shard_map/ppermute | solution.py:307
  102.4 11.3 %collective-permute-start.3 = (bf16[384,256]{1,0:T(8,128)(2,1)S(1)}, bf16[384,256]{1,0:T(8,128)(2,1)S(1)}, u32[]{:S(2)}, u32[]{:S(2)}) collective-permute-start(bf16[384,256]{1,0:T(8,128)(2,1)S(1)} %add_convert_fusion.refs_0_), channel_id=1, source_target_pairs={{0,64},{64,128},{128,192},{192,0},{1,65},{65,129},{129,193},{193,1... | collective-permute-start | bytes 589832 | tf_op jit(solution)/shard_map/ppermute | solution.py:307
  105.1 9.3 %collective-permute-start.4 = (bf16[384,256]{1,0:T(8,128)(2,1)S(1)}, bf16[384,256]{1,0:T(8,128)(2,1)S(1)}, u32[]{:S(2)}, u32[]{:S(2)}) collective-permute-start(bf16[384,256]{1,0:T(8,128)(2,1)S(1)} %add_convert_fusion.refs_0_), channel_id=1, source_target_pairs={{0,128},{64,192},{128,0},{192,64},{1,129},{65,193},{129,1},{193,65... | collective-permute-start | bytes 589832 | tf_op jit(solution)/shard_map/ppermute | solution.py:307
  105.3 11.8 %collective-permute-start.5 = (bf16[384,256]{1,0:T(8,128)(2,1)S(1)}, bf16[384,256]{1,0:T(8,128)(2,1)S(1)}, u32[]{:S(2)}, u32[]{:S(2)}) collective-permute-start(bf16[384,256]{1,0:T(8,128)(2,1)S(1)} %add_convert_fusion.refs_0_), channel_id=1, source_target_pairs={{0,192},{64,0},{128,64},{192,128},{1,193},{65,1},{129,65},{193,129... | collective-permute-start | bytes 589832 | tf_op jit(solution)/shard_map/ppermute | solution.py:307

commit v2 on v1

--- a/solution.py
+++ b/solution.py
@@ -34,7 +34,7 @@
     return lax.broadcasted_iota(jnp.int32, shape, dim)
 
 
-def table_kernel(hard_ref, easy_ref, stagger_ref, out_ref):
+def write_table(hard_ref, easy_ref, stagger_ref, out_ref):
     pulses = out_ref.shape[3] // 2
     groups = hard_ref.shape[1]
     rows = 4 * groups
@@ -47,13 +47,8 @@
         return jnp.sum(jnp.where(at, ref[...], 0), axis=1, keepdims=True)
 
     k = jnp.where(t < 2, picked(hard_ref, group), picked(easy_ref, 2 * group + t - 2))
-    spread = (iota((rows, groups), 1) == iota((rows, groups), 0) // 4).astype(jnp.float32)
-    both = jnp.dot(
-        spread.astype(jnp.bfloat16),
-        stagger_ref[...].astype(jnp.float32).astype(jnp.bfloat16),
-        preferred_element_type=jnp.float32,
-    ).astype(jnp.int32)
-    d = jnp.where(t == 0, both[:, 0:1], jnp.where(t == 1, both[:, 1:2], 0))
+    first, second = picked(stagger_ref.at[0:1], group), picked(stagger_ref.at[1:2], group)
+    d = jnp.where(t == 0, first, jnp.where(t == 1, second, 0))
     lag = iota((rows, part), 1) - d
     phase = ((k * lag) & (pulses - 1)).astype(jnp.float32) * (TWO_PI / pulses)
     c0, s0 = jnp.cos(phase), jnp.sin(phase)
@@ -74,18 +69,77 @@
         out_ref[:, 1, :, high] = real.astype(jnp.bfloat16)
 
 
-def doppler_table(hard_bins, easy_bins, stagger, pulses, groups):
-    out = pl.pallas_call(
-        table_kernel,
-        out_shape=jax.ShapeDtypeStruct((groups // 8, 2, 32, 2 * pulses), jnp.bfloat16),
-        in_specs=[vmem()] * 3,
-        out_specs=vmem(),
-        compiler_params=params(24),
+PIECES = 8
+
+
+def front_kernel(
+    hard_ref, easy_ref, stagger_ref, x_hbm, out_hbm, table, held, wide, tall, done, sems, out_sems
+):
+    lines, gates, ch = x_hbm.shape
+    piece = lines // PIECES
+    copies = []
+    for n in range(PIECES):
+        at = pl.ds(n * piece, piece)
+        copies.append(pltpu.make_async_copy(x_hbm.at[at], held.at[at], sems.at[n]))
+        copies[-1].start()
+    write_table(hard_ref, easy_ref, stagger_ref, table)
+    for n, copy in enumerate(copies):
+        copy.wait()
+        x = held[n * piece : (n + 1) * piece].astype(jnp.float32)
+        x = x.reshape(piece * gates, ch)
+        for half in range(ch // 128):
+            lanes = slice(half * 128, (half + 1) * 128)
+            wide[half, n * piece * gates : (n + 1) * piece * gates] = x[:, lanes]
+    factors = table[...].reshape(-1, lines)
+    rows = factors.shape[0]
+    for g in range(gates):
+        x = [wide[half, pl.ds(g, lines, stride=gates), :] for half in range(ch // 128)]
+        x = jnp.concatenate(x, axis=1).astype(jnp.bfloat16)
+        y = jnp.dot(factors, x, preferred_element_type=jnp.float32)
+        for half in range(ch // 128):
+            tall[half, pl.ds(g, rows, stride=gates), :] = y[:, half * 128 : (half + 1) * 128]
+    for z in range(rows // 64):
+        lines_of = slice(z * 64 * gates, (z + 1) * 64 * gates)
+        for half in range(ch // 128):
+            block = tall[half, lines_of].reshape(2, 8, 4, gates, 128)
+            block = jnp.concatenate([block[0], block[1]], axis=2).astype(jnp.bfloat16)
+            done[z * 8 : (z + 1) * 8, :, :, half * 128 : (half + 1) * 128] = block
+        at = pl.ds(z * 8, 8)
+        copies.append(pltpu.make_async_copy(done.at[at], out_hbm.at[at], out_sems.at[z]))
+        copies[-1].start()
+    for copy in copies[PIECES:]:
+        copy.wait()
+
+
+def spectra_of(hard_bins, easy_bins, stagger, cube):
+    pulses, gates, ch = cube.shape[1:]
+    groups = hard_bins.shape[0]
+    lines = 2 * pulses
+    rows = 8 * groups
+    return pl.pallas_call(
+        front_kernel,
+        out_shape=jax.ShapeDtypeStruct((groups, 4, 2 * gates, ch), jnp.bfloat16),
+        in_specs=[vmem()] * 3 + [pl.BlockSpec(memory_space=pl.ANY)],
+        out_specs=pl.BlockSpec(memory_space=pl.ANY),
+        scratch_shapes=[
+            pltpu.VMEM((groups // 8, 2, 32, lines), jnp.bfloat16),
+            pltpu.VMEM((lines, gates, ch), jnp.bfloat16),
+            pltpu.VMEM((ch // 128, lines * gates, 128), jnp.float32),
+            pltpu.VMEM((ch // 128, rows * gates, 128), jnp.float32),
+            pltpu.VMEM((groups, 4, 2 * gates, ch), jnp.bfloat16),
+            pltpu.SemaphoreType.DMA((PIECES,)),
+            pltpu.SemaphoreType.DMA((groups // 8,)),
+        ],
+        compiler_params=params(62),
         cost_estimate=pl.CostEstimate(
-            flops=10**7, bytes_accessed=MIB, transcendentals=200000
-        ),
-    )(hard_bins.reshape(1, -1), easy_bins.reshape(1, -1), stagger)
-    return out.reshape(-1, 2 * pulses)
+            flops=2 * 10**9, bytes_accessed=6 * MIB, transcendentals=200000
+        ),
+    )(
+        hard_bins.reshape(1, -1),
+        easy_bins.reshape(1, -1),
+        stagger.T,
+        cube.reshape(lines, gates, ch),
+    )
 
 
 def gram_kernel(section_ref, gates_ref, x_ref, *refs, train):
@@ -146,7 +200,7 @@
         in_specs=[pl.BlockSpec(memory_space=pltpu.SMEM), vmem(), vmem()],
         out_specs=[vmem()] * sections,
         scratch_shapes=[pltpu.VMEM((sections, *block), jnp.bfloat16)],
-        compiler_params=params(40),
+        compiler_params=params(24),
         cost_estimate=pl.CostEstimate(
             flops=2 * 10**9, bytes_accessed=4 * MIB, transcendentals=0
         ),
@@ -223,7 +277,7 @@
         in_specs=[pl.BlockSpec(memory_space=pltpu.SMEM)] + [vmem()] * (len(parts) + 2),
         out_specs=vmem(),
         scratch_shapes=[pltpu.VMEM((len(parts), *parts[0].shape), jnp.bfloat16)],
-        compiler_params=params(40),
+        compiler_params=params(24),
         cost_estimate=pl.CostEstimate(
             flops=6 * 10**9, bytes_accessed=3 * MIB, transcendentals=0
         ),
@@ -290,14 +344,6 @@
     )(y, w)
 
 
-def spectra_of(table, cube, groups):
-    pulses, gates, ch = cube.shape[1:]
-    flat = cube.reshape(2 * pulses, gates * ch)
-    out = jnp.dot(table, flat, preferred_element_type=jnp.float32).astype(jnp.bfloat16)
-    out = out.reshape(groups // 8, 2, 8, 4, gates, ch)
-    return jnp.transpose(out, (0, 2, 3, 1, 4, 5)).reshape(groups, 4, 2 * gates, ch)
-
-
 def route(spectra):
     return lax.all_to_all(spectra, "bins", split_axis=0, concat_axis=0, tiled=True)
 
@@ -308,15 +354,14 @@
 
 
 def per_device(cube_train, cube_apply, hard_bins, easy_bins, stagger, hard_gates, easy_gates):
-    groups = lax.axis_size("bins")
     section = lax.axis_index("segment")
     group = lax.axis_index("bins")
     pulses = cube_train.shape[1]
     ch = cube_train.shape[3]
-    table = doppler_table(hard_bins, easy_bins, stagger, pulses, groups)
-    train = route(spectra_of(table, cube_train, groups))
+    bins = (hard_bins, easy_bins, stagger)
+    train = route(spectra_of(*bins, cube_train))
     gates = jnp.concatenate([hard_gates, easy_gates], axis=0)
-    apply_spectra = spectra_of(table, cube_apply, groups)
+    apply_spectra = spectra_of(*bins, cube_apply)
     train, apply_spectra = lax.optimization_barrier((train, apply_spectra))
     routed = route(apply_spectra)
     sections = lax.axis_size("segment")

time: 136 us -> 131 us (0.963)
  local copies, waits for them, and re-layouts: 16.7 us -> 1.23 us
  Pallas kernels: 13 us -> 27.3 us
  matrix products: 4.74 us -> 0 us
  waiting for transfers between devices: 70.6 us -> 73.1 us
    pallas_call x1 -> x2, Pallas kernels: 1.62 us -> 14.4 us  [spectra_of(): pl.pallas_call(front_kernel, out_shape=jax.ShapeDtypeStruct((groups, 4, 2...]
    unnamed x19 -> x8, local copies, waits for them, and re-layouts: 12.4 us -> 0.03 us
    dot_general x2 -> x0, matrix products: 4.74 us -> none  [spectra_of(): jnp.dot(table, flat, preferred_element_type=jnp.float32)]
    all_to_all x2, waiting for transfers between devices: 52.2 us -> 55.3 us  [route(): lax.all_to_all(spectra, 'bins', split_axis=0, concat_axis=0, tiled=True)]
    reshape x2 -> x0, local copies, waits for them, and re-layouts: 3.01 us -> none  [spectra_of(): out = out.reshape(groups // 8, 2, 8, 4, gates, ch)]
    ppermute x6, starting transfers between devices: 7.79 us -> 6.22 us  [shifted(): lax.ppermute(x, 'segment', [(i, (i + by) % size) for i in range(size)])]
    pallas_call x1, Pallas kernels: 2.35 us -> 3.89 us  [gram(): pl.pallas_call(functools.partial(gram_kernel, train=gates.shape[1]), out_...]
  transfers between devices with their start and end apart: 8 -> 8, of which waited for: 7 -> 8; matrix products, arithmetic and copies ran while one was open for 8% -> 2% of each run, Pallas kernels for 7% -> 14%
where the time goes in v2:
time: 131 us
  waiting for transfers between devices  73.1 us (56%)
  Pallas kernels  27.3 us (21%)
  starting transfers between devices  23.9 us (18%)
  between operations  3.39 us (3%)
  other arithmetic  1.64 us (1%)
    all_to_all x2, waiting for transfers between devices, route(): lax.all_to_all(spectra, 'bins', split_axis=0, concat_axis=0, tiled=True)  55.3 us
    ppermute x6, waiting for transfers between devices, shifted(): lax.ppermute(x, 'segment', [(i, (i + by) % size) for i in range(size)])  17.8 us
    all_to_all x2, starting transfers between devices, route(): lax.all_to_all(spectra, 'bins', split_axis=0, concat_axis=0, tiled=True)  17.7 us
    pallas_call x2, Pallas kernels, spectra_of(): pl.pallas_call(front_kernel, out_shape=jax.ShapeDtypeStruct((groups, 4, 2...  14.4 us
    pallas_call x1, Pallas kernels, solve(): pl.pallas_call(solve_kernel, out_shape=jax.ShapeDtypeStruct((4, ch, 2 * B...  6.57 us
    ppermute x6, starting transfers between devices, shifted(): lax.ppermute(x, 'segment', [(i, (i + by) % size) for i in range(size)])  6.22 us
    pallas_call x1, Pallas kernels, gram(): pl.pallas_call(functools.partial(gram_kernel, train=gates.shape[1]), out_...  3.89 us
  transfers between devices with their start and end apart: 8, of which 8 were waited for; matrix products, arithmetic and copies ran while one was open for 2% of the time, Pallas kernels for 14%

profile of v2, /device:TPU:6, one launch (start us, length us, event | category | flops | bytes accessed | tf_op | source)
XLA Modules:
  0.0 130.6 jit_solution(3235486328125665221)
XLA Ops:
  0.6 7.2 %shard_map.86 = bf16[64,4,16,256]{3,2,1,0:T(8,128)(2,1)} custom-call(s32[1,64]{1,0:T(1,128)} %bitcast.15, s32[1,128]{1,0:T(1,128)} %bitcast.13, s32[2,64]{1,0:T(2,128)} %bitcast.9, bf16[1024,8,256]{2,1,0:T(8,128)(2,1)} %bitcast.11), custom_call_target="tpu_custom_call" | custom-call | flops 2000000000 | bytes 6291456 | tf_op jit(solution)/shard_map/pallas_call | solution.py:119
  7.8 12.4 %all-to-all-start = ((bf16[64,4,16,256]{3,2,1,0:T(8,128)(2,1)}), bf16[64,4,16,256]{3,2,1,0:T(8,128)(2,1)}, u32[]{:S(2)}, u32[]{:S(2)}) async-start(bf16[64,4,16,256]{3,2,1,0:T(8,128)(2,1)} %shard_map.86), calls=%async_computation | async-start | bytes 4194304 | tf_op jit(solution)/shard_map/all_to_all | solution.py:348
  20.2 7.2 %shard_map.87 = bf16[64,4,16,256]{3,2,1,0:T(8,128)(2,1)} custom-call(s32[1,64]{1,0:T(1,128)} %bitcast.16, s32[1,128]{1,0:T(1,128)} %bitcast.14, s32[2,64]{1,0:T(2,128)} %bitcast.10, bf16[1024,8,256]{2,1,0:T(8,128)(2,1)} %bitcast.12), custom_call_target="tpu_custom_call" | custom-call | flops 2000000000 | bytes 6291456 | tf_op jit(solution)/shard_map/pallas_call | solution.py:119
  27.4 0.0 copy-start.3
  27.5 0.0 copy-start.2
  27.5 0.0 copy-start
  27.5 0.0 copy-start.1
  27.5 43.9 %all-to-all-done.x_ref = bf16[64,4,16,256]{3,2,1,0:T(8,128)(2,1)} async-done(((bf16[64,4,16,256]{3,2,1,0:T(8,128)(2,1)}), bf16[64,4,16,256]{3,2,1,0:T(8,128)(2,1)}, u32[]{:S(2)}, u32[]{:S(2)}) %all-to-all-start) | async-done | bytes 2097184 | tf_op jit(solution)/shard_map/all_to_all | solution.py:348
  71.4 5.3 %all-to-all-start.1 = ((bf16[64,4,16,256]{3,2,1,0:T(8,128)(2,1)}), bf16[64,4,16,256]{3,2,1,0:T(8,128)(2,1)S(1)}, u32[]{:S(2)}, u32[]{:S(2)}) async-start(bf16[64,4,16,256]{3,2,1,0:T(8,128)(2,1)} %shard_map.87), calls=%async_computation.1 | async-start | bytes 4194304 | tf_op jit(solution)/shard_map/all_to_all | solution.py:348
  76.8 0.0 copy-done.3
  76.8 0.6 dynamic_slice.9
  77.4 0.0 copy-done.2
  77.4 0.6 constant_dynamic-slice_fusion.1
  80.6 0.0 copy-done
  80.6 0.0 copy-done.1
  80.7 3.9 %shard_map.88 = (bf16[384,256]{1,0:T(8,128)(2,1)S(1)}, bf16[384,256]{1,0:T(8,128)(2,1)S(1)}, bf16[384,256]{1,0:T(8,128)(2,1)S(1)}, bf16[384,256]{1,0:T(8,128)(2,1)S(1)}) custom-call(s32[1]{0:T(128)} %bitcast.5.section_ref, s32[3,512]{1,0:T(4,128)S(1)} %pad_add_fusion.gates_ref, bf16[64,4,16,256]{3,2,1,0:T(8,128)(2,1)} %all-to-all-done.x_ref), custom_call_target="tpu_custom_call" | custom-call | flops 2000000000 | bytes 4194304 | tf_op jit(solution)/shard_map/pallas_call | solution.py:197
  84.6 0.6 collective-permute-start
  85.1 2.4 %collective-permute-start.1 = (bf16[384,256]{1,0:T(8,128)(2,1)S(1)}, bf16[384,256]{1,0:T(8,128)(2,1)S(1)}, u32[]{:S(2)}, u32[]{:S(2)}) collective-permute-start(bf16[384,256]{1,0:T(8,128)(2,1)S(1)} %get-tuple-element.12), channel_id=1, source_target_pairs={{0,128},{64,192},{128,0},{192,64},{1,129},{65,193},{129,1},{193,65... | collective-permute-start | bytes 589832 | tf_op jit(solution)/shard_map/ppermute | solution.py:353
  87.5 0.0 collective-permute-start.2
  87.5 0.5 fusion.9
  88.1 0.9 fusion.1
  89.0 3.4 %collective-permute-done = bf16[384,256]{1,0:T(8,128)(2,1)S(1)} collective-permute-done((bf16[384,256]{1,0:T(8,128)(2,1)S(1)}, bf16[384,256]{1,0:T(8,128)(2,1)S(1)}, u32[]{:S(2)}, u32[]{:S(2)}) %collective-permute-start) | collective-permute-done | bytes 196640 | tf_op jit(solution)/shard_map/ppermute | solution.py:353
  92.4 2.0 %collective-permute-done.1 = bf16[384,256]{1,0:T(8,128)(2,1)S(1)} collective-permute-done((bf16[384,256]{1,0:T(8,128)(2,1)S(1)}, bf16[384,256]{1,0:T(8,128)(2,1)S(1)}, u32[]{:S(2)}, u32[]{:S(2)}) %collective-permute-start.1) | collective-permute-done | bytes 196640 | tf_op jit(solution)/shard_map/ppermute | solution.py:353
  94.4 3.0 %collective-permute-done.2 = bf16[384,256]{1,0:T(8,128)(2,1)S(1)} collective-permute-done((bf16[384,256]{1,0:T(8,128)(2,1)S(1)}, bf16[384,256]{1,0:T(8,128)(2,1)S(1)}, u32[]{:S(2)}, u32[]{:S(2)}) %collective-permute-start.2) | collective-permute-done | bytes 196640 | tf_op jit(solution)/shard_map/ppermute | solution.py:353
  97.4 0.1 add_convert_fusion.refs_0_
  97.5 1.0 collective-permute-start.3
  98.6 2.0 %collective-permute-start.4 = (bf16[384,256]{1,0:T(8,128)(2,1)S(1)}, bf16[384,256]{1,0:T(8,128)(2,1)S(1)}, u32[]{:S(2)}, u32[]{:S(2)}) collective-permute-start(bf16[384,256]{1,0:T(8,128)(2,1)S(1)} %add_convert_fusion.refs_0_), channel_id=1, source_target_pairs={{0,128},{64,192},{128,0},{192,64},{1,129},{65,193},{129,1},{193,65... | collective-permute-start | bytes 589832 | tf_op jit(solution)/shard_map/ppermute | solution.py:353
  100.6 0.2 collective-permute-start.5
  100.9 4.5 %collective-permute-done.3.refs_1_ = bf16[384,256]{1,0:T(8,128)(2,1)S(1)} collective-permute-done((bf16[384,256]{1,0:T(8,128)(2,1)S(1)}, bf16[384,256]{1,0:T(8,128)(2,1)S(1)}, u32[]{:S(2)}, u32[]{:S(2)}) %collective-permute-start.3) | collective-permute-done | bytes 196640 | tf_op jit(solution)/shard_map/ppermute | solution.py:353
  105.4 2.5 %collective-permute-done.4.refs_2_ = bf16[384,256]{1,0:T(8,128)(2,1)S(1)} collective-permute-done((bf16[384,256]{1,0:T(8,128)(2,1)S(1)}, bf16[384,256]{1,0:T(8,128)(2,1)S(1)}, u32[]{:S(2)}, u32[]{:S(2)}) %collective-permute-start.4) | collective-permute-done | bytes 196640 | tf_op jit(solution)/shard_map/ppermute | solution.py:353
  107.9 2.3 %collective-permute-done.5.refs_3_ = bf16[384,256]{1,0:T(8,128)(2,1)S(1)} collective-permute-done((bf16[384,256]{1,0:T(8,128)(2,1)S(1)}, bf16[384,256]{1,0:T(8,128)(2,1)S(1)}, u32[]{:S(2)}, u32[]{:S(2)}) %collective-permute-start.5) | collective-permute-done | bytes 196640 | tf_op jit(solution)/shard_map/ppermute | solution.py:353
  110.2 6.6 %shard_map.89.w_ref = bf16[4,256,256]{2,1,0:T(8,128)(2,1)S(1)} custom-call(s32[1]{0:T(128)} %bitcast.5.section_ref, bf16[384,256]{1,0:T(8,128)(2,1)S(1)} %add_convert_fusion.refs_0_, bf16[384,256]{1,0:T(8,128)(2,1)S(1)} %collective-permute-done.3.refs_1_, bf16[384,256]{1,0:T(8,128)(2,1)S(1)} %collective-permute-done.4.refs_2_, ...), custom_call_target="tpu_custom_call" | custom-call | flops 6000000000 | bytes 3145728 | tf_op jit(solution)/shard_map/pallas_call | solution.py:274
  116.8 11.4 %all-to-all-done.1.y_ref = bf16[64,4,16,256]{3,2,1,0:T(8,128)(2,1)S(1)} async-done(((bf16[64,4,16,256]{3,2,1,0:T(8,128)(2,1)}), bf16[64,4,16,256]{3,2,1,0:T(8,128)(2,1)S(1)}, u32[]{:S(2)}, u32[]{:S(2)}) %all-to-all-start.1) | async-done | bytes 2097184 | tf_op jit(solution)/shard_map/all_to_all | solution.py:348
  128.1 2.4 %shard_map.90 = (f32[1,2,512,128]{3,2,1,0:T(8,128)}, f32[2,2,512,128]{3,2,1,0:T(8,128)}) custom-call(bf16[64,4,16,256]{3,2,1,0:T(8,128)(2,1)S(1)} %all-to-all-done.1.y_ref, bf16[4,256,256]{2,1,0:T(8,128)(2,1)S(1)} %shard_map.89.w_ref), custom_call_target="tpu_custom_call" | custom-call | flops 500000000 | bytes 4194304 | tf_op jit(solution)/shard_map/pallas_call | solution.py:325
  (4 shorter events, 0.1 us)
Async XLA Ops:
  7.8 63.6 %all-to-all-start = ((bf16[64,4,16,256]{3,2,1,0:T(8,128)(2,1)}), bf16[64,4,16,256]{3,2,1,0:T(8,128)(2,1)}, u32[]{:S(2)}, u32[]{:S(2)}) async-start(bf16[64,4,16,256]{3,2,1,0:T(8,128)(2,1)} %shard_map.86), calls=%async_computation | async-start | bytes 4194304 | tf_op jit(solution)/shard_map/all_to_all | solution.py:348
  27.4 49.3 %copy-start.3 = (s32[64]{0:T(128)S(1)}, s32[64]{0:T(128)}, u32[]{:S(2)}) copy-start(s32[64]{0:T(128)} %param.9) | copy-start | bytes 772
  27.5 49.9 %copy-start.2 = (s32[64,2]{0,1:T(2,128)S(1)}, s32[64,2]{0,1:T(2,128)}, u32[]{:S(2)}) copy-start(s32[64,2]{0,1:T(2,128)} %param.11) | copy-start | bytes 1540
  27.5 53.2 %copy-start = (s32[2,512]{1,0:T(2,128)S(1)}, s32[2,512]{1,0:T(2,128)}, u32[]{:S(2)}) copy-start(s32[2,512]{1,0:T(2,128)} %param.13) | copy-start | bytes 12292
  27.5 53.2 %copy-start.1 = (s32[1,512]{1,0:T(1,128)S(1)}, s32[1,512]{1,0:T(1,128)}, u32[]{:S(2)}) copy-start(s32[1,512]{1,0:T(1,128)} %param.12) | copy-start | bytes 6148
  71.4 56.7 %all-to-all-start.1 = ((bf16[64,4,16,256]{3,2,1,0:T(8,128)(2,1)}), bf16[64,4,16,256]{3,2,1,0:T(8,128)(2,1)S(1)}, u32[]{:S(2)}, u32[]{:S(2)}) async-start(bf16[64,4,16,256]{3,2,1,0:T(8,128)(2,1)} %shard_map.87), calls=%async_computation.1 | async-start | bytes 4194304 | tf_op jit(solution)/shard_map/all_to_all | solution.py:348
  84.6 7.8 %collective-permute-start = (bf16[384,256]{1,0:T(8,128)(2,1)S(1)}, bf16[384,256]{1,0:T(8,128)(2,1)S(1)}, u32[]{:S(2)}, u32[]{:S(2)}) collective-permute-start(bf16[384,256]{1,0:T(8,128)(2,1)S(1)} %get-tuple-element.11), channel_id=1, source_target_pairs={{0,64},{64,128},{128,192},{192,0},{1,65},{65,129},{129,193},{193,1... | collective-permute-start | bytes 589832 | tf_op jit(solution)/shard_map/ppermute | solution.py:353
  85.1 9.3 %collective-permute-start.1 = (bf16[384,256]{1,0:T(8,128)(2,1)S(1)}, bf16[384,256]{1,0:T(8,128)(2,1)S(1)}, u32[]{:S(2)}, u32[]{:S(2)}) collective-permute-start(bf16[384,256]{1,0:T(8,128)(2,1)S(1)} %get-tuple-element.12), channel_id=1, source_target_pairs={{0,128},{64,192},{128,0},{192,64},{1,129},{65,193},{129,1},{193,65... | collective-permute-start | bytes 589832 | tf_op jit(solution)/shard_map/ppermute | solution.py:353
  87.5 9.9 %collective-permute-start.2 = (bf16[384,256]{1,0:T(8,128)(2,1)S(1)}, bf16[384,256]{1,0:T(8,128)(2,1)S(1)}, u32[]{:S(2)}, u32[]{:S(2)}) collective-permute-start(bf16[384,256]{1,0:T(8,128)(2,1)S(1)} %get-tuple-element.13), channel_id=1, source_target_pairs={{0,192},{64,0},{128,64},{192,128},{1,193},{65,1},{129,65},{193,129... | collective-permute-start | bytes 589832 | tf_op jit(solution)/shard_map/ppermute | solution.py:353
  97.5 7.8 %collective-permute-start.3 = (bf16[384,256]{1,0:T(8,128)(2,1)S(1)}, bf16[384,256]{1,0:T(8,128)(2,1)S(1)}, u32[]{:S(2)}, u32[]{:S(2)}) collective-permute-start(bf16[384,256]{1,0:T(8,128)(2,1)S(1)} %add_convert_fusion.refs_0_), channel_id=1, source_target_pairs={{0,64},{64,128},{128,192},{192,0},{1,65},{65,129},{129,193},{193,1... | collective-permute-start | bytes 589832 | tf_op jit(solution)/shard_map/ppermute | solution.py:353
  98.6 9.3 %collective-permute-start.4 = (bf16[384,256]{1,0:T(8,128)(2,1)S(1)}, bf16[384,256]{1,0:T(8,128)(2,1)S(1)}, u32[]{:S(2)}, u32[]{:S(2)}) collective-permute-start(bf16[384,256]{1,0:T(8,128)(2,1)S(1)} %add_convert_fusion.refs_0_), channel_id=1, source_target_pairs={{0,128},{64,192},{128,0},{192,64},{1,129},{65,193},{129,1},{193,65... | collective-permute-start | bytes 589832 | tf_op jit(solution)/shard_map/ppermute | solution.py:353
  100.6 9.6 %collective-permute-start.5 = (bf16[384,256]{1,0:T(8,128)(2,1)S(1)}, bf16[384,256]{1,0:T(8,128)(2,1)S(1)}, u32[]{:S(2)}, u32[]{:S(2)}) collective-permute-start(bf16[384,256]{1,0:T(8,128)(2,1)S(1)} %add_convert_fusion.refs_0_), channel_id=1, source_target_pairs={{0,192},{64,0},{128,64},{192,128},{1,193},{65,1},{129,65},{193,129... | collective-permute-start | bytes 589832 | tf_op jit(solution)/shard_map/ppermute | solution.py:353

commit v3 on v2

--- a/solution.py
+++ b/solution.py
@@ -299,44 +299,56 @@
     return jnp.concatenate([jnp.cos(angle), jnp.sin(angle)], axis=1) * scale
 
 
-def beam_kernel(y_ref, w_ref, hard_ref, easy_ref):
-    sources = y_ref.shape[0]
-    rows = sources * 16
-
-    def product(t):
-        y = y_ref[:, t].reshape(rows, -1)
-        return jnp.dot(y, w_ref[t], preferred_element_type=jnp.float32)
+def beam_kernel(y_ref, w_ref, hard_hbm, easy_hbm, hard, easy, sems, *, blocks):
+    step = y_ref.shape[0] // blocks
+    copies = []
 
     def parts(p):
-        p = p.reshape(sources, 2, 8, 2 * BEAMS)
+        p = p.reshape(step, 2, 8, 2 * BEAMS)
         real = p[:, 0, :, :BEAMS] + p[:, 1, :, BEAMS:]
         imag = p[:, 1, :, :BEAMS] - p[:, 0, :, BEAMS:]
-        return real.reshape(sources * 8, BEAMS), imag.reshape(sources * 8, BEAMS)
-
-    hard_ref[0, 0], hard_ref[0, 1] = parts(product(0) + product(1))
-    for e in range(2):
-        easy_ref[e, 0], easy_ref[e, 1] = parts(product(2 + e))
+        return real.reshape(step * 8, BEAMS), imag.reshape(step * 8, BEAMS)
+
+    for n in range(blocks):
+
+        def product(t):
+            y = y_ref[n * step : (n + 1) * step, t].reshape(step * 16, -1)
+            return jnp.dot(y, w_ref[t], preferred_element_type=jnp.float32)
+
+        gates = slice(n * step * 8, (n + 1) * step * 8)
+        at = pl.ds(n * step * 8, step * 8)
+        hard[0, 0, gates], hard[0, 1, gates] = parts(product(0) + product(1))
+        copies.append(
+            pltpu.make_async_copy(hard.at[:, :, at], hard_hbm.at[:, :, at], sems.at[0, n])
+        )
+        copies[-1].start()
+        for e in range(2):
+            easy[e, 0, gates], easy[e, 1, gates] = parts(product(2 + e))
+        copies.append(
+            pltpu.make_async_copy(easy.at[:, :, at], easy_hbm.at[:, :, at], sems.at[1, n])
+        )
+        copies[-1].start()
+    for copy in copies:
+        copy.wait()
 
 
 def beams(y, w, blocks=4):
-    sources, _, _, ch = y.shape
-    step = sources // blocks
-    gates = sources * 8
+    gates = y.shape[0] * 8
+    hard = (1, 2, gates, BEAMS)
+    easy = (2, 2, gates, BEAMS)
     return pl.pallas_call(
-        beam_kernel,
-        grid=(blocks,),
+        functools.partial(beam_kernel, blocks=blocks),
         out_shape=(
-            jax.ShapeDtypeStruct((1, 2, gates, BEAMS), jnp.float32),
-            jax.ShapeDtypeStruct((2, 2, gates, BEAMS), jnp.float32),
+            jax.ShapeDtypeStruct(hard, jnp.float32),
+            jax.ShapeDtypeStruct(easy, jnp.float32),
         ),
-        in_specs=[
-            pl.BlockSpec((step, 4, 16, ch), lambda i: (i, 0, 0, 0)),
-            pl.BlockSpec((4, ch, 2 * BEAMS), lambda i: (0, 0, 0)),
+        in_specs=[vmem()] * 2,
+        out_specs=(pl.BlockSpec(memory_space=pl.ANY), pl.BlockSpec(memory_space=pl.ANY)),
+        scratch_shapes=[
+            pltpu.VMEM(hard, jnp.float32),
+            pltpu.VMEM(easy, jnp.float32),
+            pltpu.SemaphoreType.DMA((2, blocks)),
         ],
-        out_specs=(
-            pl.BlockSpec((1, 2, step * 8, BEAMS), lambda i: (0, 0, i, 0)),
-            pl.BlockSpec((2, 2, step * 8, BEAMS), lambda i: (0, 0, i, 0)),
-        ),
         compiler_params=params(24),
         cost_estimate=pl.CostEstimate(
             flops=5 * 10**8, bytes_accessed=4 * MIB, transcendentals=0

time: 131 us -> 130 us (level)
  no operation moved by 1% of the time
where the time goes in v3:
time: 130 us
  waiting for transfers between devices  73.1 us (56%)
  Pallas kernels  26.4 us (20%)
  starting transfers between devices  23.9 us (18%)
  between operations  3.57 us (3%)
  other arithmetic  1.64 us (1%)
    all_to_all x2, waiting for transfers between devices, route(): lax.all_to_all(spectra, 'bins', split_axis=0, concat_axis=0, tiled=True)  55.3 us
    ppermute x6, waiting for transfers between devices, shifted(): lax.ppermute(x, 'segment', [(i, (i + by) % size) for i in range(size)])  17.8 us
    all_to_all x2, starting transfers between devices, route(): lax.all_to_all(spectra, 'bins', split_axis=0, concat_axis=0, tiled=True)  17.7 us
    pallas_call x2, Pallas kernels, spectra_of(): pl.pallas_call(front_kernel, out_shape=jax.ShapeDtypeStruct((groups, 4, 2...  14.4 us
    pallas_call x1, Pallas kernels, solve(): pl.pallas_call(solve_kernel, out_shape=jax.ShapeDtypeStruct((4, ch, 2 * B...  6.57 us
    ppermute x6, starting transfers between devices, shifted(): lax.ppermute(x, 'segment', [(i, (i + by) % size) for i in range(size)])  6.22 us
    pallas_call x1, Pallas kernels, gram(): pl.pallas_call(functools.partial(gram_kernel, train=gates.shape[1]), out_...  3.89 us
  transfers between devices with their start and end apart: 8, of which 8 were waited for; matrix products, arithmetic and copies ran while one was open for 2% of the time, Pallas kernels for 14%

profile of v3, /device:TPU:6, one launch (start us, length us, event | category | flops | bytes accessed | tf_op | source)
XLA Modules:
  0.0 129.9 jit_solution(10887720040789915393)
XLA Ops:
  0.6 7.2 %shard_map.86 = bf16[64,4,16,256]{3,2,1,0:T(8,128)(2,1)} custom-call(s32[1,64]{1,0:T(1,128)} %bitcast.15, s32[1,128]{1,0:T(1,128)} %bitcast.13, s32[2,64]{1,0:T(2,128)} %bitcast.9, bf16[1024,8,256]{2,1,0:T(8,128)(2,1)} %bitcast.11), custom_call_target="tpu_custom_call" | custom-call | flops 2000000000 | bytes 6291456 | tf_op jit(solution)/shard_map/pallas_call | solution.py:119
  7.8 12.4 %all-to-all-start = ((bf16[64,4,16,256]{3,2,1,0:T(8,128)(2,1)}), bf16[64,4,16,256]{3,2,1,0:T(8,128)(2,1)}, u32[]{:S(2)}, u32[]{:S(2)}) async-start(bf16[64,4,16,256]{3,2,1,0:T(8,128)(2,1)} %shard_map.86), calls=%async_computation | async-start | bytes 4194304 | tf_op jit(solution)/shard_map/all_to_all | solution.py:360
  20.2 7.2 %shard_map.87 = bf16[64,4,16,256]{3,2,1,0:T(8,128)(2,1)} custom-call(s32[1,64]{1,0:T(1,128)} %bitcast.16, s32[1,128]{1,0:T(1,128)} %bitcast.14, s32[2,64]{1,0:T(2,128)} %bitcast.10, bf16[1024,8,256]{2,1,0:T(8,128)(2,1)} %bitcast.12), custom_call_target="tpu_custom_call" | custom-call | flops 2000000000 | bytes 6291456 | tf_op jit(solution)/shard_map/pallas_call | solution.py:119
  27.4 0.0 copy-start.3
  27.5 0.0 copy-start.2
  27.5 0.0 copy-start
  27.5 0.0 copy-start.1
  27.5 43.9 %all-to-all-done.x_ref = bf16[64,4,16,256]{3,2,1,0:T(8,128)(2,1)} async-done(((bf16[64,4,16,256]{3,2,1,0:T(8,128)(2,1)}), bf16[64,4,16,256]{3,2,1,0:T(8,128)(2,1)}, u32[]{:S(2)}, u32[]{:S(2)}) %all-to-all-start) | async-done | bytes 2097184 | tf_op jit(solution)/shard_map/all_to_all | solution.py:360
  71.4 5.3 %all-to-all-start.1 = ((bf16[64,4,16,256]{3,2,1,0:T(8,128)(2,1)}), bf16[64,4,16,256]{3,2,1,0:T(8,128)(2,1)S(1)}, u32[]{:S(2)}, u32[]{:S(2)}) async-start(bf16[64,4,16,256]{3,2,1,0:T(8,128)(2,1)} %shard_map.87), calls=%async_computation.1 | async-start | bytes 4194304 | tf_op jit(solution)/shard_map/all_to_all | solution.py:360
  76.8 0.0 copy-done.3
  76.8 0.6 dynamic_slice.9
  77.4 0.0 copy-done.2
  77.4 0.6 constant_dynamic-slice_fusion.1
  80.6 0.0 copy-done
  80.6 0.0 copy-done.1
  80.7 3.9 %shard_map.88 = (bf16[384,256]{1,0:T(8,128)(2,1)S(1)}, bf16[384,256]{1,0:T(8,128)(2,1)S(1)}, bf16[384,256]{1,0:T(8,128)(2,1)S(1)}, bf16[384,256]{1,0:T(8,128)(2,1)S(1)}) custom-call(s32[1]{0:T(128)} %bitcast.5.section_ref, s32[3,512]{1,0:T(4,128)S(1)} %pad_add_fusion.gates_ref, bf16[64,4,16,256]{3,2,1,0:T(8,128)(2,1)} %all-to-all-done.x_ref), custom_call_target="tpu_custom_call" | custom-call | flops 2000000000 | bytes 4194304 | tf_op jit(solution)/shard_map/pallas_call | solution.py:197
  84.6 0.6 collective-permute-start
  85.1 2.4 %collective-permute-start.1 = (bf16[384,256]{1,0:T(8,128)(2,1)S(1)}, bf16[384,256]{1,0:T(8,128)(2,1)S(1)}, u32[]{:S(2)}, u32[]{:S(2)}) collective-permute-start(bf16[384,256]{1,0:T(8,128)(2,1)S(1)} %get-tuple-element.12), channel_id=1, source_target_pairs={{0,128},{64,192},{128,0},{192,64},{1,129},{65,193},{129,1},{193,65... | collective-permute-start | bytes 589832 | tf_op jit(solution)/shard_map/ppermute | solution.py:365
  87.5 0.0 collective-permute-start.2
  87.5 0.5 fusion.9
  88.1 0.9 fusion.1
  89.0 3.4 %collective-permute-done = bf16[384,256]{1,0:T(8,128)(2,1)S(1)} collective-permute-done((bf16[384,256]{1,0:T(8,128)(2,1)S(1)}, bf16[384,256]{1,0:T(8,128)(2,1)S(1)}, u32[]{:S(2)}, u32[]{:S(2)}) %collective-permute-start) | collective-permute-done | bytes 196640 | tf_op jit(solution)/shard_map/ppermute | solution.py:365
  92.4 2.0 %collective-permute-done.1 = bf16[384,256]{1,0:T(8,128)(2,1)S(1)} collective-permute-done((bf16[384,256]{1,0:T(8,128)(2,1)S(1)}, bf16[384,256]{1,0:T(8,128)(2,1)S(1)}, u32[]{:S(2)}, u32[]{:S(2)}) %collective-permute-start.1) | collective-permute-done | bytes 196640 | tf_op jit(solution)/shard_map/ppermute | solution.py:365
  94.4 3.0 %collective-permute-done.2 = bf16[384,256]{1,0:T(8,128)(2,1)S(1)} collective-permute-done((bf16[384,256]{1,0:T(8,128)(2,1)S(1)}, bf16[384,256]{1,0:T(8,128)(2,1)S(1)}, u32[]{:S(2)}, u32[]{:S(2)}) %collective-permute-start.2) | collective-permute-done | bytes 196640 | tf_op jit(solution)/shard_map/ppermute | solution.py:365
  97.4 0.1 add_convert_fusion.refs_0_
  97.5 1.0 collective-permute-start.3
  98.6 2.0 %collective-permute-start.4 = (bf16[384,256]{1,0:T(8,128)(2,1)S(1)}, bf16[384,256]{1,0:T(8,128)(2,1)S(1)}, u32[]{:S(2)}, u32[]{:S(2)}) collective-permute-start(bf16[384,256]{1,0:T(8,128)(2,1)S(1)} %add_convert_fusion.refs_0_), channel_id=1, source_target_pairs={{0,128},{64,192},{128,0},{192,64},{1,129},{65,193},{129,1},{193,65... | collective-permute-start | bytes 589832 | tf_op jit(solution)/shard_map/ppermute | solution.py:365
  100.6 0.2 collective-permute-start.5
  100.9 4.5 %collective-permute-done.3.refs_1_ = bf16[384,256]{1,0:T(8,128)(2,1)S(1)} collective-permute-done((bf16[384,256]{1,0:T(8,128)(2,1)S(1)}, bf16[384,256]{1,0:T(8,128)(2,1)S(1)}, u32[]{:S(2)}, u32[]{:S(2)}) %collective-permute-start.3) | collective-permute-done | bytes 196640 | tf_op jit(solution)/shard_map/ppermute | solution.py:365
  105.4 2.5 %collective-permute-done.4.refs_2_ = bf16[384,256]{1,0:T(8,128)(2,1)S(1)} collective-permute-done((bf16[384,256]{1,0:T(8,128)(2,1)S(1)}, bf16[384,256]{1,0:T(8,128)(2,1)S(1)}, u32[]{:S(2)}, u32[]{:S(2)}) %collective-permute-start.4) | collective-permute-done | bytes 196640 | tf_op jit(solution)/shard_map/ppermute | solution.py:365
  107.9 2.3 %collective-permute-done.5.refs_3_ = bf16[384,256]{1,0:T(8,128)(2,1)S(1)} collective-permute-done((bf16[384,256]{1,0:T(8,128)(2,1)S(1)}, bf16[384,256]{1,0:T(8,128)(2,1)S(1)}, u32[]{:S(2)}, u32[]{:S(2)}) %collective-permute-start.5) | collective-permute-done | bytes 196640 | tf_op jit(solution)/shard_map/ppermute | solution.py:365
  110.2 6.6 %shard_map.89.w_ref = bf16[4,256,256]{2,1,0:T(8,128)(2,1)S(1)} custom-call(s32[1]{0:T(128)} %bitcast.5.section_ref, bf16[384,256]{1,0:T(8,128)(2,1)S(1)} %add_convert_fusion.refs_0_, bf16[384,256]{1,0:T(8,128)(2,1)S(1)} %collective-permute-done.3.refs_1_, bf16[384,256]{1,0:T(8,128)(2,1)S(1)} %collective-permute-done.4.refs_2_, ...), custom_call_target="tpu_custom_call" | custom-call | flops 6000000000 | bytes 3145728 | tf_op jit(solution)/shard_map/pallas_call | solution.py:274
  116.8 11.4 %all-to-all-done.1.y_ref = bf16[64,4,16,256]{3,2,1,0:T(8,128)(2,1)S(1)} async-done(((bf16[64,4,16,256]{3,2,1,0:T(8,128)(2,1)}), bf16[64,4,16,256]{3,2,1,0:T(8,128)(2,1)S(1)}, u32[]{:S(2)}, u32[]{:S(2)}) %all-to-all-start.1) | async-done | bytes 2097184 | tf_op jit(solution)/shard_map/all_to_all | solution.py:360
  128.1 1.5 %shard_map.90 = (f32[1,2,512,128]{3,2,1,0:T(8,128)}, f32[2,2,512,128]{3,2,1,0:T(8,128)}) custom-call(bf16[64,4,16,256]{3,2,1,0:T(8,128)(2,1)S(1)} %all-to-all-done.1.y_ref, bf16[4,256,256]{2,1,0:T(8,128)(2,1)S(1)} %shard_map.89.w_ref), custom_call_target="tpu_custom_call" | custom-call | flops 500000000 | bytes 4194304 | tf_op jit(solution)/shard_map/pallas_call | solution.py:339
  (4 shorter events, 0.1 us)
Async XLA Ops:
  7.8 63.6 %all-to-all-start = ((bf16[64,4,16,256]{3,2,1,0:T(8,128)(2,1)}), bf16[64,4,16,256]{3,2,1,0:T(8,128)(2,1)}, u32[]{:S(2)}, u32[]{:S(2)}) async-start(bf16[64,4,16,256]{3,2,1,0:T(8,128)(2,1)} %shard_map.86), calls=%async_computation | async-start | bytes 4194304 | tf_op jit(solution)/shard_map/all_to_all | solution.py:360
  27.4 49.3 %copy-start.3 = (s32[64]{0:T(128)S(1)}, s32[64]{0:T(128)}, u32[]{:S(2)}) copy-start(s32[64]{0:T(128)} %param.9) | copy-start | bytes 772
  27.5 49.9 %copy-start.2 = (s32[64,2]{0,1:T(2,128)S(1)}, s32[64,2]{0,1:T(2,128)}, u32[]{:S(2)}) copy-start(s32[64,2]{0,1:T(2,128)} %param.11) | copy-start | bytes 1540
  27.5 53.2 %copy-start = (s32[2,512]{1,0:T(2,128)S(1)}, s32[2,512]{1,0:T(2,128)}, u32[]{:S(2)}) copy-start(s32[2,512]{1,0:T(2,128)} %param.13) | copy-start | bytes 12292
  27.5 53.2 %copy-start.1 = (s32[1,512]{1,0:T(1,128)S(1)}, s32[1,512]{1,0:T(1,128)}, u32[]{:S(2)}) copy-start(s32[1,512]{1,0:T(1,128)} %param.12) | copy-start | bytes 6148
  71.4 56.7 %all-to-all-start.1 = ((bf16[64,4,16,256]{3,2,1,0:T(8,128)(2,1)}), bf16[64,4,16,256]{3,2,1,0:T(8,128)(2,1)S(1)}, u32[]{:S(2)}, u32[]{:S(2)}) async-start(bf16[64,4,16,256]{3,2,1,0:T(8,128)(2,1)} %shard_map.87), calls=%async_computation.1 | async-start | bytes 4194304 | tf_op jit(solution)/shard_map/all_to_all | solution.py:360
  84.6 7.8 %collective-permute-start = (bf16[384,256]{1,0:T(8,128)(2,1)S(1)}, bf16[384,256]{1,0:T(8,128)(2,1)S(1)}, u32[]{:S(2)}, u32[]{:S(2)}) collective-permute-start(bf16[384,256]{1,0:T(8,128)(2,1)S(1)} %get-tuple-element.11), channel_id=1, source_target_pairs={{0,64},{64,128},{128,192},{192,0},{1,65},{65,129},{129,193},{193,1... | collective-permute-start | bytes 589832 | tf_op jit(solution)/shard_map/ppermute | solution.py:365
  85.1 9.3 %collective-permute-start.1 = (bf16[384,256]{1,0:T(8,128)(2,1)S(1)}, bf16[384,256]{1,0:T(8,128)(2,1)S(1)}, u32[]{:S(2)}, u32[]{:S(2)}) collective-permute-start(bf16[384,256]{1,0:T(8,128)(2,1)S(1)} %get-tuple-element.12), channel_id=1, source_target_pairs={{0,128},{64,192},{128,0},{192,64},{1,129},{65,193},{129,1},{193,65... | collective-permute-start | bytes 589832 | tf_op jit(solution)/shard_map/ppermute | solution.py:365
  87.5 9.9 %collective-permute-start.2 = (bf16[384,256]{1,0:T(8,128)(2,1)S(1)}, bf16[384,256]{1,0:T(8,128)(2,1)S(1)}, u32[]{:S(2)}, u32[]{:S(2)}) collective-permute-start(bf16[384,256]{1,0:T(8,128)(2,1)S(1)} %get-tuple-element.13), channel_id=1, source_target_pairs={{0,192},{64,0},{128,64},{192,128},{1,193},{65,1},{129,65},{193,129... | collective-permute-start | bytes 589832 | tf_op jit(solution)/shard_map/ppermute | solution.py:365
  97.5 7.8 %collective-permute-start.3 = (bf16[384,256]{1,0:T(8,128)(2,1)S(1)}, bf16[384,256]{1,0:T(8,128)(2,1)S(1)}, u32[]{:S(2)}, u32[]{:S(2)}) collective-permute-start(bf16[384,256]{1,0:T(8,128)(2,1)S(1)} %add_convert_fusion.refs_0_), channel_id=1, source_target_pairs={{0,64},{64,128},{128,192},{192,0},{1,65},{65,129},{129,193},{193,1... | collective-permute-start | bytes 589832 | tf_op jit(solution)/shard_map/ppermute | solution.py:365
  98.6 9.3 %collective-permute-start.4 = (bf16[384,256]{1,0:T(8,128)(2,1)S(1)}, bf16[384,256]{1,0:T(8,128)(2,1)S(1)}, u32[]{:S(2)}, u32[]{:S(2)}) collective-permute-start(bf16[384,256]{1,0:T(8,128)(2,1)S(1)} %add_convert_fusion.refs_0_), channel_id=1, source_target_pairs={{0,128},{64,192},{128,0},{192,64},{1,129},{65,193},{129,1},{193,65... | collective-permute-start | bytes 589832 | tf_op jit(solution)/shard_map/ppermute | solution.py:365
  100.6 9.6 %collective-permute-start.5 = (bf16[384,256]{1,0:T(8,128)(2,1)S(1)}, bf16[384,256]{1,0:T(8,128)(2,1)S(1)}, u32[]{:S(2)}, u32[]{:S(2)}) collective-permute-start(bf16[384,256]{1,0:T(8,128)(2,1)S(1)} %add_convert_fusion.refs_0_), channel_id=1, source_target_pairs={{0,192},{64,0},{128,64},{192,128},{1,193},{65,1},{129,65},{193,129... | collective-permute-start | bytes 589832 | tf_op jit(solution)/shard_map/ppermute | solution.py:365
